TPU v7x, 32 devices: a whole 2x2x4 slice. The times are simulated.
32 devices in a mesh: pipe: 2 (over core), dp: 16 (over z, y, x).
Axes of the slice: x: 2, y: 2, z: 4, core: 2. Of those that a mesh axis runs over, the one named last changes fastest.
Arguments:
- hidden_in: bfloat16 [2, 16, 256, 1024], P(None, 'dp'), may hold values from -6 to 6
- lengths: int32 [2, 16], P(None, 'dp'), may hold values from 200 to 256, as said below
- out_grad: bfloat16 [2, 16, 256, 1024], P(None, 'dp'), may hold values from -6 to 6
- w_qkv: bfloat16 [2, 1024, 3072], P('pipe', 'dp'), may hold values from -0.1875 to 0.1875
- w_out: bfloat16 [2, 1024, 1024], P('pipe', 'dp'), may hold values from -1.5 to 1.5
- w_up: bfloat16 [2, 1024, 4096], P('pipe', 'dp'), may hold values from -0.1875 to 0.1875
- w_down: bfloat16 [2, 4096, 1024], P('pipe', 'dp'), may hold values from -0.09375 to 0.09375
- vectors: bfloat16 [2, 10, 1024], P('pipe', None, 'dp'), may hold values from -0.41 to 1.41
- up_bias: bfloat16 [2, 4096], P('pipe', 'dp'), may hold values from -3 to 3
Outputs:
- edges: float32 [2, 2, 16, 256, 1024], P('pipe', None, 'dp')
- grad_qkv: float32 [2, 1024, 3072], P('pipe', 'dp')
- grad_out: float32 [2, 1024, 1024], P('pipe', 'dp')
- grad_up: float32 [2, 1024, 4096], P('pipe', 'dp')
- grad_down: float32 [2, 4096, 1024], P('pipe', 'dp')
- grad_vectors: float32 [2, 10, 1024], P('pipe', None, 'dp')
- grad_up_bias: float32 [2, 4096], P('pipe', 'dp')
Inputs may be any that keep to these rules, and one draw needn't show every extreme that they name: `lengths`: in each micro-batch one utterance has exactly 256 units.
All inputs are finite; a program needn't handle non-finite values.
Results may differ from a plain program's by a relative error of at most 0.011.
Values may be sent and summed in bfloat16 or wider, within the bound.
A program may use at most 448 MiB of HBM per device.

v0:
```python
import jax
import jax.numpy as jnp
from jax import lax
from jax.sharding import PartitionSpec as P

D = 1024
HEADS = 16
HEAD_DIM = 64
FF = 4096
SEQ = 256
MICRO = 2


EPS = 1e-05


def passed_along(value, axis, steps):
    count = lax.axis_size(axis)
    leading, last = (max(0, -steps), min(count, count - steps))
    return lax.ppermute(value, axis, [(source, source + steps) for source in range(leading, last)])


def norm_parts(values):
    center = values - jnp.mean(values, -1, keepdims=True)
    factor = lax.rsqrt(jnp.mean(center * center, -1, keepdims=True) + EPS)
    return (center * factor, factor)


def norm_back(grad_normed, normed, factor):
    return factor * (
        grad_normed
        - jnp.mean(grad_normed, -1, keepdims=True)
        - normed * jnp.mean(grad_normed * normed, -1, keepdims=True)
    )


def gelu_exact(values):
    return jax.nn.gelu(values, approximate=False)


def pieces(inputs, length, weights, is_last):
    w_qkv, w_out, w_up, w_down, vectors, up_bias = weights
    row_count = inputs.shape[0]
    positions = jnp.arange(row_count, dtype=jnp.int32)
    valid_rows = (positions < length).astype(jnp.float32)[:, None]
    allowed = (positions[None, :] <= positions[:, None]) & (positions[None, :] < length)
    vec_rows = vectors.astype(jnp.float32)
    normed_one, factor_one = norm_parts(inputs)
    attn_in = (normed_one * vec_rows[0] + vec_rows[1]).astype(jnp.bfloat16)
    projected = jnp.dot(attn_in, w_qkv, preferred_element_type=jnp.float32)
    query_heads = (
        (projected[:, :D] + vec_rows[2]).astype(jnp.bfloat16).reshape(row_count, HEADS, HEAD_DIM)
    )
    key_heads = projected[:, D : 2 * D].astype(jnp.bfloat16).reshape(row_count, HEADS, HEAD_DIM)
    value_heads = (
        (projected[:, 2 * D :] + vec_rows[3])
        .astype(jnp.bfloat16)
        .reshape(row_count, HEADS, HEAD_DIM)
    )
    scores = jnp.einsum(
        "qhd,khd->hqk", query_heads, key_heads, preferred_element_type=jnp.float32
    ) * HEAD_DIM ** (-0.5)
    scores = jnp.where(allowed[None], scores, -1e30)
    row_peak = jnp.max(scores, -1, keepdims=True)
    logsum = row_peak + jnp.log(jnp.sum(jnp.exp(scores - row_peak), -1, keepdims=True))
    attn_probs = jnp.exp(scores - logsum)
    probs_low = attn_probs.astype(jnp.bfloat16)
    attended = jnp.einsum(
        "hqk,khd->qhd", probs_low, value_heads, preferred_element_type=jnp.float32
    )
    attended = attended.reshape(row_count, D).astype(jnp.bfloat16)
    hidden = inputs + jnp.dot(attended, w_out, preferred_element_type=jnp.float32) + vec_rows[4]
    normed_two, factor_two = norm_parts(hidden)
    ffn_in = (normed_two * vec_rows[5] + vec_rows[6]).astype(jnp.bfloat16)
    up_value = jnp.dot(ffn_in, w_up, preferred_element_type=jnp.float32) + up_bias.astype(
        jnp.float32
    )
    activated = gelu_exact(up_value).astype(jnp.bfloat16)
    summed = hidden + jnp.dot(activated, w_down, preferred_element_type=jnp.float32) + vec_rows[7]
    normed_three, factor_three = norm_parts(summed)
    result = jnp.where(is_last, normed_three * vec_rows[8] + vec_rows[9], summed) * valid_rows
    return (
        result,
        valid_rows,
        vec_rows,
        normed_one,
        factor_one,
        attn_in,
        query_heads,
        key_heads,
        value_heads,
        attn_probs,
        probs_low,
        attended,
        normed_two,
        factor_two,
        ffn_in,
        up_value,
        activated,
        normed_three,
        factor_three,
    )


def forward(inputs, length, weights, is_last):
    return pieces(inputs, length, weights, is_last)[0]


def backward(inputs, length, weights, is_last, cotangent):
    w_qkv, w_out, w_up, w_down, vectors, up_bias = weights
    (
        result,
        valid_rows,
        vec_rows,
        normed_one,
        factor_one,
        attn_in,
        query_heads,
        key_heads,
        value_heads,
        attn_probs,
        probs_low,
        attended,
        normed_two,
        factor_two,
        ffn_in,
        up_value,
        activated,
        normed_three,
        factor_three,
    ) = pieces(inputs, length, weights, is_last)
    row_count = inputs.shape[0]
    grad_z = cotangent * valid_rows
    grad_final_gain = jnp.where(is_last, jnp.sum(grad_z * normed_three, 0), 0.0)
    grad_final_bias = jnp.where(is_last, jnp.sum(grad_z, 0), 0.0)
    grad_y = jnp.where(is_last, norm_back(grad_z * vec_rows[8], normed_three, factor_three), grad_z)
    grad_branch = grad_y.astype(jnp.bfloat16)
    grad_down_bias = jnp.sum(grad_branch.astype(jnp.float32), 0)
    grad_down = jnp.einsum("sf,sd->fd", activated, grad_branch, preferred_element_type=jnp.float32)
    grad_act = jnp.einsum("sd,fd->sf", grad_branch, w_down, preferred_element_type=jnp.float32)
    unused, gelu_pull = jax.vjp(gelu_exact, up_value)
    grad_upper = gelu_pull(grad_act)[0].astype(jnp.bfloat16)
    grad_upper_bias = jnp.sum(grad_upper.astype(jnp.float32), 0)
    grad_up = jnp.einsum("sd,sf->df", ffn_in, grad_upper, preferred_element_type=jnp.float32)
    grad_ffn_in = jnp.einsum("sf,df->sd", grad_upper, w_up, preferred_element_type=jnp.float32)
    grad_gain_two = jnp.sum(grad_ffn_in * normed_two, 0)
    grad_bias_two = jnp.sum(grad_ffn_in, 0)
    grad_hidden = grad_y + norm_back(grad_ffn_in * vec_rows[5], normed_two, factor_two)
    grad_attn = grad_hidden.astype(jnp.bfloat16)
    grad_out_bias = jnp.sum(grad_attn.astype(jnp.float32), 0)
    grad_out = jnp.einsum("sa,sd->ad", attended, grad_attn, preferred_element_type=jnp.float32)
    grad_mixed = jnp.einsum("sd,ad->sa", grad_attn, w_out, preferred_element_type=jnp.float32)
    grad_mixed = grad_mixed.astype(jnp.bfloat16).reshape(row_count, HEADS, HEAD_DIM)
    grad_probs = jnp.einsum(
        "qhd,khd->hqk", grad_mixed, value_heads, preferred_element_type=jnp.float32
    )
    grad_value = jnp.einsum(
        "hqk,qhd->khd", probs_low, grad_mixed, preferred_element_type=jnp.float32
    )
    grad_scores = attn_probs * (grad_probs - jnp.sum(grad_probs * attn_probs, -1, keepdims=True))
    grad_scores = grad_scores.astype(jnp.bfloat16)
    grad_query = jnp.einsum(
        "hqk,khd->qhd", grad_scores, key_heads, preferred_element_type=jnp.float32
    ) * HEAD_DIM ** (-0.5)
    grad_key = jnp.einsum(
        "hqk,qhd->khd", grad_scores, query_heads, preferred_element_type=jnp.float32
    ) * HEAD_DIM ** (-0.5)
    grad_proj = jnp.concatenate(
        [
            grad_query.reshape(row_count, D),
            grad_key.reshape(row_count, D),
            grad_value.reshape(row_count, D),
        ],
        axis=1,
    ).astype(jnp.bfloat16)
    grad_proj_wide = grad_proj.astype(jnp.float32)
    grad_query_bias = jnp.sum(grad_proj_wide[:, :D], 0)
    grad_value_bias = jnp.sum(grad_proj_wide[:, 2 * D :], 0)
    grad_qkv = jnp.einsum("sd,se->de", attn_in, grad_proj, preferred_element_type=jnp.float32)
    grad_attn_in = jnp.einsum("se,de->sd", grad_proj, w_qkv, preferred_element_type=jnp.float32)
    grad_gain_one = jnp.sum(grad_attn_in * normed_one, 0)
    grad_bias_one = jnp.sum(grad_attn_in, 0)
    grad_inputs = grad_hidden + norm_back(grad_attn_in * vec_rows[0], normed_one, factor_one)
    grad_vec = jnp.stack(
        [
            grad_gain_one,
            grad_bias_one,
            grad_query_bias,
            grad_value_bias,
            grad_out_bias,
            grad_gain_two,
            grad_bias_two,
            grad_down_bias,
            grad_final_gain,
            grad_final_bias,
        ]
    )
    return (grad_inputs, (grad_qkv, grad_out, grad_up, grad_down, grad_vec, grad_upper_bias))


def per_device(hidden_in, lengths, out_grad, w_qkv, w_out, w_up, w_down, vectors, up_bias):
    section = lax.axis_index("pipe")
    is_last = section == 1
    shards = (w_qkv, w_out, w_up, w_down, vectors, up_bias)
    full_shapes = ((D, 3 * D), (D, D), (D, FF), (FF, D), (10, D), (FF,))
    incoming = jnp.zeros((SEQ, D), jnp.bfloat16)
    saved_inputs = []
    results = []
    for step_index in range(MICRO + 1):
        micro_now = step_index - section
        active = (micro_now >= 0) & (micro_now < MICRO)
        micro_slot = jnp.clip(micro_now, 0, MICRO - 1)
        fetched = (
            lax.all_gather(shards[0], "dp", axis=1, tiled=True),
            lax.all_gather(shards[1], "dp", axis=1, tiled=True),
            lax.all_gather(shards[2], "dp", axis=1, tiled=True),
            lax.all_gather(shards[3], "dp", axis=1, tiled=True),
            lax.all_gather(shards[4], "dp", axis=2, tiled=True),
            lax.all_gather(shards[5], "dp", axis=1, tiled=True),
        )
        current = tuple((member[0] for member in fetched))
        own_input = hidden_in[min(step_index, MICRO - 1), 0].astype(jnp.float32)
        section_input = jnp.where(section == 0, own_input, incoming.astype(jnp.float32))
        length = lengths[micro_slot, 0]
        result = lax.cond(
            active,
            lambda: forward(section_input, length, current, is_last),
            lambda: jnp.zeros((SEQ, D), jnp.float32),
        )
        saved_inputs.append(section_input)
        results.append(result)
        if step_index < MICRO:
            incoming = passed_along(result.astype(jnp.bfloat16), "pipe", 1)
    running = tuple((jnp.zeros(member.shape[1:], jnp.float32) for member in shards))
    returning = jnp.zeros((SEQ, D), jnp.bfloat16)
    input_grads = []
    for step_index in range(MICRO + 1):
        micro_now = MICRO - step_index - section
        active = (micro_now >= 0) & (micro_now < MICRO)
        micro_slot = jnp.clip(micro_now, 0, MICRO - 1)
        fetched = (
            lax.all_gather(shards[0], "dp", axis=1, tiled=True),
            lax.all_gather(shards[1], "dp", axis=1, tiled=True),
            lax.all_gather(shards[2], "dp", axis=1, tiled=True),
            lax.all_gather(shards[3], "dp", axis=1, tiled=True),
            lax.all_gather(shards[4], "dp", axis=2, tiled=True),
            lax.all_gather(shards[5], "dp", axis=1, tiled=True),
        )
        current = tuple((member[0] for member in fetched))
        cotangent = jnp.where(
            section == 1, out_grad[micro_slot, 0].astype(jnp.float32), returning.astype(jnp.float32)
        )
        length = lengths[micro_slot, 0]
        section_input = saved_inputs[MICRO - step_index]
        grad_inputs, grads_now = lax.cond(
            active,
            lambda: backward(section_input, length, current, is_last, cotangent),
            lambda: (
                jnp.zeros((SEQ, D), jnp.float32),
                tuple((jnp.zeros(shape_full, jnp.float32) for shape_full in full_shapes)),
            ),
        )
        input_grads.append(grad_inputs)
        if step_index < MICRO:
            returning = passed_along(grad_inputs.astype(jnp.bfloat16), "pipe", -1)
        scattered = (
            lax.psum_scatter(grads_now[0], "dp", scatter_dimension=0, tiled=True),
            lax.psum_scatter(grads_now[1], "dp", scatter_dimension=0, tiled=True),
            lax.psum_scatter(grads_now[2], "dp", scatter_dimension=0, tiled=True),
            lax.psum_scatter(grads_now[3], "dp", scatter_dimension=0, tiled=True),
            lax.psum_scatter(grads_now[4], "dp", scatter_dimension=1, tiled=True),
            lax.psum_scatter(grads_now[5], "dp", scatter_dimension=0, tiled=True),
        )
        running = tuple((total + term for total, term in zip(running, scattered)))
    paired = [
        jnp.where(section == 0, input_grads[MICRO - micro_index], results[micro_index + 1])
        for micro_index in range(MICRO)
    ]
    edges = jnp.stack(paired)[None, :, None]
    return (
        edges,
        running[0][None],
        running[1][None],
        running[2][None],
        running[3][None],
        running[4][None],
        running[5][None],
    )


def solution(mesh):
    placed = (
        P(None, "dp", None, None),
        P(None, "dp"),
        P(None, "dp", None, None),
        P("pipe", "dp", None),
        P("pipe", "dp", None),
        P("pipe", "dp", None),
        P("pipe", "dp", None),
        P("pipe", None, "dp"),
        P("pipe", "dp"),
    )
    return jax.shard_map(
        per_device,
        mesh=mesh,
        in_specs=placed,
        out_specs=(
            P("pipe", None, "dp", None, None),
            P("pipe", "dp", None),
            P("pipe", "dp", None),
            P("pipe", "dp", None),
            P("pipe", "dp", None),
            P("pipe", None, "dp"),
            P("pipe", "dp"),
        ),
        check_vma=False,
    )
```

profile of v0, /device:TPU:0, one launch (start us, length us, event | category | flops | bytes accessed | tf_op | source)
XLA Modules:
  0.0 1938.8 jit_solution(9920529745725133077)
XLA Ops:
  10.8 45.9 %all_gather.12 = bf16[1,10,1024]{1,0,2:T(2,128)(2,1)S(1)} all-gather(bf16[1,10,64]{1,0,2:T(2,128)(2,1)S(1)} %copy.180), channel_id=1, replica_groups=mesh['pipe'=2,'dp'=16] {'dp'}, dimensions={2}, use_global_device_ids=true | all-gather | bytes 21760 | tf_op jit(solution)/shard_map/all_gather | solution.py:246
  57.0 36.0 %all_gather.16 = bf16[1,4096]{1,0:T(2,128)(2,1)S(1)} all-gather(bf16[1,256]{1,0:T(2,128)(2,1)} %param.29), channel_id=1, replica_groups=mesh['pipe'=2,'dp'=16] {'dp'}, dimensions={1}, use_global_device_ids=true | all-gather | bytes 8704 | tf_op jit(solution)/shard_map/all_gather | solution.py:247
  96.6 74.5 %all-gather.5.cloned.1.call-done = bf16[1,1024,3072]{2,1,0:T(8,128)(2,1)} async-done(((bf16[1,64,3072]{2,1,0:T(8,128)(2,1)}), bf16[1,1024,3072]{2,1,0:T(8,128)(2,1)}) %all-gather.5.cloned.1.call-update) | async-done | bytes 6291472 | tf_op jit(solution)/shard_map/all_gather | solution.py:242
  171.1 113.9 %all-gather.9.cloned.1.call-done = bf16[1,1024,4096]{2,1,0:T(8,128)(2,1)} async-done(((bf16[1,64,4096]{2,1,0:T(8,128)(2,1)}), bf16[1,1024,4096]{2,1,0:T(8,128)(2,1)}) %all-gather.9.cloned.1.call-update) | async-done | bytes 8388624 | tf_op jit(solution)/shard_map/all_gather | solution.py:244
  285.0 113.7 %all-gather.11.cloned.1.call-done = bf16[1,4096,1024]{2,1,0:T(8,128)(2,1)} async-done(((bf16[1,256,1024]{2,1,0:T(8,128)(2,1)}), bf16[1,4096,1024]{2,1,0:T(8,128)(2,1)}) %all-gather.11.cloned.1.call-update) | async-done | bytes 8388624 | tf_op jit(solution)/shard_map/all_gather | solution.py:245
  398.6 39.4 %conditional.6 = (bf16[256,1024]{1,0:T(8,128)(2,1)}) conditional(s32[]{:T(128)} %convert_element_type.467, () %tuple.58, (pred[]{:T(512)}, f32[256,1024]{1,0:T(8,128)}, bf16[10,1024]{1,0:T(8,128)(2,1)S(1)}, bf16[1024,3072]{1,0:T(8,128)(2,1)}, s32[]{:T(128)}, /*index=5*/bf16[1024,1024]{1,0:T(8,128)(2,1)}, bf16[1024,4096]{1,0:T(8,128)(2,1)}, ...), branch_computations={%region_0.1_spmd, %region_1.10_spmd} | conditional | flops 6801720832 | bytes 85505640 | solution.py:225
  417.2 18.8 fusion.447
  442.3 37.9 %conditional.7 = (f32[256,1024]{1,0:T(8,128)S(1)}) conditional(s32[]{:T(128)} %convert_element_type.469, () %tuple.61, (pred[]{:T(512)}, f32[256,1024]{1,0:T(8,128)}, bf16[10,1024]{1,0:T(8,128)(2,1)S(1)}, bf16[1024,3072]{1,0:T(8,128)(2,1)}, s32[]{:T(128)}, /*index=5*/bf16[1024,1024]{1,0:T(8,128)(2,1)}, bf16[1024,4096]{1,0:T(8,128)(2,1)}, ...), branch_computations={%region_10.11_spmd, %region_11.20_spmd} | conditional | flops 6801458688 | bytes 86029928 | solution.py:225
  460.9 18.7 fusion.450
  485.3 34.1 %conditional.8 = (bf16[256,1024]{1,0:T(8,128)(2,1)}, f32[1024,3072]{1,0:T(8,128)}, f32[1024,1024]{1,0:T(8,128)}, f32[1024,4096]{1,0:T(8,128)}, f32[4096,1024]{1,...) conditional(s32[]{:T(128)} %convert_element_type.474, () %tuple.60, (pred[]{:T(512)}, ...), branch_computations={%region_20.21_spmd, %region_21.48_spmd} | conditional | flops 20290848768 | bytes 434658656 | solution.py:255
  520.8 8.8 conditional.11
  529.6 59.9 %collective-permute-done.2 = bf16[256,1024]{1,0:T(8,128)(2,1)} collective-permute-done((bf16[256,1024]{1,0:T(8,128)(2,1)}, bf16[256,1024]{1,0:T(8,128)(2,1)}, u32[]{:S(2)}, u32[]{:S(2)}) %collective-permute-start.2) | collective-permute-done | bytes 524320 | tf_op jit(solution)/shard_map/ppermute | solution.py:20
  590.6 107.9 %conditional.9 = (f32[256,1024]{1,0:T(8,128)}, f32[1024,3072]{1,0:T(8,128)}, f32[1024,1024]{1,0:T(8,128)}, f32[1024,4096]{1,0:T(8,128)}, f32[4096,1024]{1,0:T(8,...) conditional(s32[]{:T(128)} %convert_element_type.469, () %tuple.57, (pred[]{:T(512)}, f32[256,1024]{1,0:T(8,128)}, ...), branch_computations={%region_48.49_spmd, %region_49.76_spmd} | conditional | flops 20289798144 | bytes 429412640 | solution.py:255
  613.5 16.6 multiply_convert_fusion.3
  634.8 11.3 convert_reduce_fusion.3
  670.7 8.1 fusion.292
  681.5 8.2 fusion.295
  702.8 37.6 %collective-permute-done.3 = bf16[256,1024]{1,0:T(8,128)(2,1)S(1)} collective-permute-done((bf16[256,1024]{1,0:T(8,128)(2,1)S(1)}, bf16[256,1024]{1,0:T(8,128)(2,1)S(1)}, u32[]{:S(2)}, u32[]{:S(2)}) %collective-permute-start.3) | collective-permute-done | bytes 524320 | tf_op jit(solution)/shard_map/ppermute | solution.py:20
  741.6 104.0 %conditional.10 = (f32[256,1024]{1,0:T(8,128)}, f32[1024,3072]{1,0:T(8,128)}, f32[1024,1024]{1,0:T(8,128)}, f32[1024,4096]{1,0:T(8,128)}, f32[4096,1024]{1,0:T(8...) conditional(s32[]{:T(128)} %convert_element_type.467, () %tuple.56, (pred[]{:T(512)}, f32[256,1024]{1,0:T(8,128)}, ...), branch_computations={%region_76.77_spmd, %region_77.104_spmd} | conditional | flops 20289798144 | bytes 427315584 | solution.py:255
  763.7 13.2 multiply_convert_fusion.5
  781.5 11.4 convert_reduce_fusion.6
  828.2 8.2 fusion.332
  836.4 8.2 fusion.317
  846.7 8.6 add_add_fusion.3
  855.4 19.1 add_add_fusion.2
  874.6 23.4 %add_add_fusion.1 = f32[1024,4096]{1,0:T(8,128)} fusion(f32[1024,4096]{1,0:T(8,128)} %get-tuple-element.336, f32[1024,4096]{1,0:T(8,128)} %get-tuple-element.334, f32[1024,4096]{1,0:T(8,128)} %get-tuple-element.335), kind=kLoop, calls=%fused_computation.706 | loop fusion | flops 8388608 | bytes 67108864 | tf_op jit(solution)/shard_map/add | solution.py:274
  898.1 24.0 %add_add_fusion = f32[4096,1024]{1,0:T(8,128)} fusion(f32[4096,1024]{1,0:T(8,128)} %get-tuple-element.339, f32[4096,1024]{1,0:T(8,128)} %get-tuple-element.337, f32[4096,1024]{1,0:T(8,128)} %get-tuple-element.338), kind=kLoop, calls=%fused_computation.705 | loop fusion | flops 8388608 | bytes 67108864 | tf_op jit(solution)/shard_map/add | solution.py:274
  923.9 74.5 %all-reduce = f32[4096]{0:T(1024)S(1)} all-reduce(f32[4096]{0:T(1024)S(1)} %add_add_fusion.5), channel_id=19, replica_groups=mesh['pipe'=2,'dp'=16] {'dp'}, use_global_device_ids=true, to_apply=%region_129.130.clone | all-reduce | flops 4096 | bytes 32768
  1003.4 13.8 reduce-scatter.10.cloned.1.call-done
  1017.2 210.8 %reduce-scatter.8.cloned.1.call-done = f32[64,3072]{1,0:T(8,128)} async-done(((f32[1024,3072]{1,0:T(8,128)}), f32[64,3072]{1,0:T(8,128)}) %reduce-scatter.8.cloned.1.call-update) | async-done | bytes 786448 | tf_op jit(solution)/shard_map/reduce_scatter | solution.py:267
  1228.0 348.9 %reduce-scatter.12.cloned.1.call-done = f32[64,4096]{1,0:T(8,128)} async-done(((f32[1024,4096]{1,0:T(8,128)}), f32[64,4096]{1,0:T(8,128)}) %reduce-scatter.12.cloned.1.call-update) | async-done | bytes 1048592 | tf_op jit(solution)/shard_map/reduce_scatter | solution.py:269
  1576.9 354.9 %reduce-scatter.14.cloned.1.call-done = f32[256,1024]{1,0:T(8,128)} async-done(((f32[4096,1024]{1,0:T(8,128)}), f32[256,1024]{1,0:T(8,128)}) %reduce-scatter.14.cloned.1.call-update) | async-done | bytes 1048592 | tf_op jit(solution)/shard_map/reduce_scatter | solution.py:270
  (356 shorter events, 222.3 us)
Async XLA Ops:
  7.2 89.4 %all-gather.7.cloned.1.call-start = ((), (), s32[]{:S(2)}) async-start(), calls=%async_computation.6 | async-start | bytes 2228224 | tf_op jit(solution)/shard_map/all_gather | solution.py:243
  7.9 163.2 %all-gather.5.cloned.1.call-start = ((), (), s32[]{:S(2)}) async-start(), calls=%async_computation.5 | async-start | bytes 6684672 | tf_op jit(solution)/shard_map/all_gather | solution.py:242
  8.6 276.3 %all-gather.9.cloned.1.call-start = ((), (), s32[]{:S(2)}) async-start(), calls=%async_computation.7 | async-start | bytes 8912896 | tf_op jit(solution)/shard_map/all_gather | solution.py:244
  9.4 389.3 %all-gather.11.cloned.1.call-start = ((), (), s32[]{:S(2)}) async-start(), calls=%async_computation.8 | async-start | bytes 8912896 | tf_op jit(solution)/shard_map/all_gather | solution.py:245
  10.0 992.0 %reduce-scatter.16.cloned.1.call-start = ((), (), s32[]{:S(2)}) async-start(), calls=%async_computation.13 | async-start | bytes 557056
  398.6 42.5 %copy-start.43 = (bf16[2,1,256,1024]{3,2,1,0:T(8,128)(2,1)S(1)}, bf16[2,1,256,1024]{3,2,1,0:T(8,128)(2,1)}, u32[]{:S(2)}) copy-start(bf16[2,1,256,1024]{3,2,1,0:T(8,128)(2,1)} %param.21) | copy-start | bytes 3145732
  438.1 3.0 collective-permute-start
  442.3 43.0 %copy-start.32 = (bf16[2,1,256,1024]{3,2,1,0:T(8,128)(2,1)S(1)}, bf16[2,1,256,1024]{3,2,1,0:T(8,128)(2,1)}, u32[]{:S(2)}) copy-start(bf16[2,1,256,1024]{3,2,1,0:T(8,128)(2,1)} %param.23) | copy-start | bytes 3145732
  480.3 3.8 collective-permute-start.1
  519.5 70.0 %collective-permute-start.2 = (bf16[256,1024]{1,0:T(8,128)(2,1)}, bf16[256,1024]{1,0:T(8,128)(2,1)}, u32[]{:S(2)}, u32[]{:S(2)}) collective-permute-start(bf16[256,1024]{1,0:T(8,128)(2,1)} %get-tuple-element.325), channel_id=1, source_target_pairs={{16,0},{17,1},{18,2},{19,3},{20,4},{21,5},{22,6},{23,7},{24,8},{25... | collective-permute-start | bytes 1572872 | tf_op jit(solution)/shard_map/ppermute | solution.py:20
  520.8 69.8 %copy-start.33 = (bf16[2,1,256,1024]{3,2,1,0:T(8,128)(2,1)S(1)}, bf16[2,1,256,1024]{3,2,1,0:T(8,128)(2,1)}, u32[]{:S(2)}) copy-start(bf16[2,1,256,1024]{3,2,1,0:T(8,128)(2,1)} %param.23) | copy-start | bytes 3145732
  609.0 21.1 %copy-start.64 = (bf16[16,64,256]{2,1,0:T(8,128)(2,1)}, bf16[16,64,256]{2,1,0:T(8,128)(2,1)S(1)}, u32[]{:S(2)}) copy-start(bf16[16,64,256]{2,1,0:T(8,128)(2,1)S(1)} %convolution_convert_fusion.5) | copy-start | bytes 1572868 | tf_op jit(solution)/shard_map/cond
  610.8 19.3 slice-start.8
  613.5 16.6 slice-start.9
  670.7 8.1 copy-start.65
  681.5 8.2 copy-start.38
  698.5 43.0 %copy-start.77 = (f32[4096]{0:T(1024)}, f32[4096]{0:T(1024)S(1)}, u32[]{:S(2)}) copy-start(f32[4096]{0:T(1024)S(1)} %get-tuple-element.344) | copy-start | bytes 49156
  698.6 43.0 %copy-start = (bf16[1,1024,1024]{2,1,0:T(8,128)(2,1)S(1)}, bf16[1,1024,1024]{2,1,0:T(8,128)(2,1)}, u32[]{:S(2)}) copy-start(bf16[1,1024,1024]{2,1,0:T(8,128)(2,1)} %all-gather.7.cloned.1.call-done) | copy-start | bytes 6291460
  701.5 38.9 %collective-permute-start.3 = (bf16[256,1024]{1,0:T(8,128)(2,1)S(1)}, bf16[256,1024]{1,0:T(8,128)(2,1)S(1)}, u32[]{:S(2)}, u32[]{:S(2)}) collective-permute-start(bf16[256,1024]{1,0:T(8,128)(2,1)S(1)} %get-tuple-element.630), channel_id=1, source_target_pairs={{16,0},{17,1},{18,2},{19,3},{20,4},{21,5},{22,6},{23,7},{24,8},{25... | collective-permute-start | bytes 1572872 | tf_op jit(solution)/shard_map/ppermute | solution.py:20
  741.5 104.0 %copy-start.74 = (f32[10,1024]{1,0:T(8,128)S(1)}, f32[10,1024]{1,0:T(8,128)}, u32[]{:S(2)}) copy-start(f32[10,1024]{1,0:T(8,128)} %copy-done.73) | copy-start | bytes 122884
  760.3 16.5 slice-start.10
  763.7 13.2 slice-start.11
  781.5 18.3 copy-start.16
  817.4 8.0 copy-start.67
  828.2 8.2 copy-start.17
  828.2 8.2 copy-start.40
  846.7 170.5 %reduce-scatter.10.cloned.1.call-start = ((), (), s32[]{:S(2)}) async-start(), calls=%async_computation.10 | async-start | bytes 4456448 | tf_op jit(solution)/shard_map/reduce_scatter | solution.py:268
  855.4 372.7 %reduce-scatter.8.cloned.1.call-start = ((), (), s32[]{:S(2)}) async-start(), calls=%async_computation.9 | async-start | bytes 13369344 | tf_op jit(solution)/shard_map/reduce_scatter | solution.py:267
  874.5 702.4 %reduce-scatter.12.cloned.1.call-start = ((), (), s32[]{:S(2)}) async-start(), calls=%async_computation.11 | async-start | bytes 17825792 | tf_op jit(solution)/shard_map/reduce_scatter | solution.py:269
  898.0 1033.8 %reduce-scatter.14.cloned.1.call-start = ((), (), s32[]{:S(2)}) async-start(), calls=%async_computation.12 | async-start | bytes 17825792 | tf_op jit(solution)/shard_map/reduce_scatter | solution.py:270
  922.0 77.0 %copy-start.19 = (f32[256,1024]{1,0:T(8,128)S(1)}, f32[256,1024]{1,0:T(8,128)}, u32[]{:S(2)}) copy-start(f32[256,1024]{1,0:T(8,128)} %copy-done.18) | copy-start | bytes 3145732
  922.0 78.4 %copy-start.36 = (f32[1,256,1024]{2,1,0:T(8,128)S(1)}, f32[1,256,1024]{2,1,0:T(8,128)}, u32[]{:S(2)}) copy-start(f32[1,256,1024]{2,1,0:T(8,128)} %get-tuple-element.631) | copy-start | bytes 3145732
  (52 other events, 152.4 us)
Sparse Core Ops, SparseCore 0:
  10.8 64.6 all-gather.6
  78.2 92.8 all-gather.4
  173.8 111.0 all-gather.8
  287.6 111.0 all-gather.10
  846.8 74.7 reduce-scatter.15
  924.4 92.7 reduce-scatter.9
  1024.4 203.5 reduce-scatter.7
  1230.9 345.9 reduce-scatter.11
  1579.8 351.9 reduce-scatter.13
where the time goes:
time: 1950 us; the launch traced here: 1940 us
  waiting for transfers between devices  1330 us (68%)
  matrix products  222 us (11%)
  blocking collectives  156 us (8%)
  other arithmetic  124 us (6%)
  local copies, waits for them, and re-layouts  61.9 us (3%)
    reduce_scatter x1, waiting for transfers between devices, per_device(): lax.psum_scatter(grads_now[3], 'dp', scatter_dimension=0, tiled=True)  355 us
    reduce_scatter x1, waiting for transfers between devices, per_device(): lax.psum_scatter(grads_now[2], 'dp', scatter_dimension=0, tiled=True)  349 us
    reduce_scatter x1, waiting for transfers between devices, per_device(): lax.psum_scatter(grads_now[0], 'dp', scatter_dimension=0, tiled=True)  211 us
    all_gather x1, waiting for transfers between devices, per_device(): lax.all_gather(shards[2], 'dp', axis=1, tiled=True)  114 us
    all_gather x1, waiting for transfers between devices, per_device(): lax.all_gather(shards[3], 'dp', axis=1, tiled=True)  114 us
    ppermute x4, waiting for transfers between devices, passed_along(): lax.ppermute(value, axis, [(source, source + steps) for source in range(l...  101 us
    add x6, other arithmetic, per_device(): running = tuple((total + term for total, term in zip(running, scattered)))  75.1 us
    unnamed x1, blocking collectives  74.5 us
  transfers between devices with their start and end apart: 13, of which 11 were waited for; matrix products, arithmetic and copies ran while one was open for 4% of the time, Pallas kernels for 0%

commit v1 on v0

v1 whole, which is shorter than its diff:
```python
import functools

import jax
import jax.numpy as jnp
from jax import lax
from jax.experimental import pallas as pl
from jax.experimental.pallas import tpu as pltpu
from jax.sharding import PartitionSpec as P

D = 1024
HEADS = 16
HEAD_DIM = 64
FF = 4096
SEQ = 256
EPS = 1e-05
MESH = pl.DeviceIdType.MESH
UNIT = 1024
HALF = UNIT // 2
UNITS = [(0, 0), (0, 1), (0, 2), (1, 0), (2, 0), (2, 1), (2, 2), (2, 3), (3, 0), (3, 1), (3, 2), (3, 3)]
BACK = [(3, 0), (2, 0), (3, 1), (2, 1), (3, 2), (2, 2), (3, 3), (2, 3), (1, 0), (0, 0), (0, 1), (0, 2)]
NU = len(UNITS)


def axis_orders(dims):
    if dims == 4:
        first, second = (3, 0, 1, 2), (2, 0, 1, 3)
        return [first, second, (0, 1, 3, 2), first, second, (0, 1, 2, 3)]
    turned = [tuple((i + 2 * turn) % dims for i in range(dims)) for turn in range(3)]
    return turned + turned


def place(dims):
    core, here = lax.axis_index("pipe"), lax.axis_index("dp")
    bits = [lax.rem(lax.div(here, 2 ** (dims - 1 - i)), 2) for i in range(dims)]
    partners = [(core, here + (1 - 2 * bits[i]) * 2 ** (dims - 1 - i)) for i in range(dims)]
    return core, bits, partners


def greet(core, here, partners):
    barrier = pltpu.get_barrier_semaphore()
    everyone = [(1 - core, here)] + partners
    for device in everyone:
        pl.semaphore_signal(barrier, inc=1, device_id=device, device_id_type=MESH)
    pl.semaphore_wait(barrier, len(everyone))


def part(ref, lead, where, matrix, block, column_half):
    if matrix == 3:
        columns = pl.ds(pl.multiple_of(column_half * HALF, HALF), HALF)
        return ref.at[lead + where + (block, slice(None), columns)]
    columns = pl.ds(pl.multiple_of(block * UNIT + column_half * HALF, HALF), HALF)
    return ref.at[lead + where + (slice(None), columns)]


def gather_kernel(dims, *refs):
    shards, small = refs[:4], refs[4]
    whole, small_all = refs[5:9], refs[9]
    local_sem, first_send, first_recv, send_sem, recv_sem, pass_send, pass_recv, small_send, small_recv = refs[10:]
    core, bits, partners = place(dims)
    here = lax.axis_index("dp")
    other = (1 - core, here)
    greet(core, here, partners)
    orders = axis_orders(dims)
    own = tuple(bits)
    total = 2 * NU

    def remote(source, target, send, recv, device):
        return pltpu.make_async_remote_copy(
            src_ref=source, dst_ref=target, send_sem=send, recv_sem=recv, device_id=device, device_id_type=MESH
        )

    def first_local(u, layer):
        matrix, block = UNITS[u]
        return pltpu.make_async_copy(
            part(shards[matrix], (), (), matrix, block, core),
            part(whole[matrix], (layer,), own, matrix, block, core),
            local_sem.at[u],
        )

    def first_remote(u, layer):
        matrix, block = UNITS[u]
        return remote(
            part(shards[matrix], (), (), matrix, block, 1 - core),
            part(whole[matrix], (layer,), own, matrix, block, 1 - core),
            first_send.at[u],
            first_recv.at[u],
            other,
        )

    def step(v, k):
        layer, u = v // NU, v % NU
        matrix, block = UNITS[u]
        order = orders[v % len(orders)]
        where = tuple(slice(None) if i in order[:k] else bits[i] for i in range(dims))
        ref = part(whole[matrix], (layer,), where, matrix, block, core)
        return remote(ref, ref, send_sem.at[v, k], recv_sem.at[v, k], partners[order[k]])

    def passing(v):
        layer, u = v // NU, v % NU
        matrix, block = UNITS[u]
        ref = part(whole[matrix], (layer,), (slice(None),) * dims, matrix, block, core)
        return remote(ref, ref, pass_send.at[v], pass_recv.at[v], other)

    small_own = pltpu.make_async_copy(small, small_all.at[(core,) + own], small_send.at[dims + 1])
    small_own.start()
    for layer in range(2):

        @pl.when(core == layer)
        def _():
            for u in range(NU):
                first_remote(u, layer).start()
                first_local(u, layer).start()

    small_own.wait()
    for k in range(dims):
        where = tuple(slice(None) if i < k else bits[i] for i in range(dims))
        ref = small_all.at[(core,) + where]
        copy = remote(ref, ref, small_send.at[k], small_recv.at[k], partners[k])
        copy.start()
        copy.wait()
    copy = remote(small_all.at[core], small_all.at[core], small_send.at[dims], small_recv.at[dims], other)
    copy.start()
    copy.wait()

    def arrive(v):
        layer, u = v // NU, v % NU

        @pl.when(core == layer)
        def _():
            first_local(u, layer).wait()
            first_remote(u, layer).wait_send()

        @pl.when(core != layer)
        def _():
            first_remote(u, layer).wait_recv()

    for tick in range(total + dims + 2):
        for k in range(dims + 1, -1, -1):
            v = tick - k
            if not 0 <= v < total:
                continue
            if k == 0:
                arrive(v)
            if 0 < k <= dims:
                step(v, k - 1).wait()
            if k < dims:
                step(v, k).start()
            if k == dims:
                passing(v).start()
            if k == dims + 1:
                passing(v).wait()


def gather(shards, small, dims):
    rows = small.shape[0]
    lead = (2,) + (2,) * dims
    shapes = [lead + s.shape for s in shards[:3]]
    shapes.append(lead + (4, shards[3].shape[0] // 4, D))
    shards = list(shards[:3]) + [shards[3].reshape(4, shards[3].shape[0] // 4, D)]
    outs = [jax.ShapeDtypeStruct(s, jnp.bfloat16) for s in shapes]
    outs.append(jax.ShapeDtypeStruct(lead + (rows, 128), small.dtype))
    dma = pltpu.SemaphoreType.DMA
    return pl.pallas_call(
        functools.partial(gather_kernel, dims),
        out_shape=outs,
        in_specs=[pl.BlockSpec(memory_space=pl.ANY)] * 5,
        out_specs=[pl.BlockSpec(memory_space=pl.ANY)] * 5,
        scratch_shapes=[
            dma((NU,)),
            dma((NU,)),
            dma((NU,)),
            dma((2 * NU, dims)),
            dma((2 * NU, dims)),
            dma((2 * NU,)),
            dma((2 * NU,)),
            dma((dims + 2,)),
            dma((dims + 1,)),
        ],
        compiler_params=pltpu.CompilerParams(collective_id=1, has_side_effects=True, vmem_limit_bytes=56 << 20),
        name="gather",
    )(*shards, small)


SLOTS = 6


def scatter_kernel(dims, *refs):
    grads, small = refs[:4], refs[4]
    outs, small_out = refs[5:9], refs[9]
    held, boxes, result, small_held, small_box = refs[10], refs[11 : 12 + dims], refs[12 + dims], refs[13 + dims], refs[14 + dims]
    load_sem, send_sem, recv_sem, credit, out_sem, end_send, end_recv, small_send, small_recv = refs[15 + dims :]
    core, bits, partners = place(dims)
    here = lax.axis_index("dp")
    other = (1 - core, here)
    greet(core, here, partners)
    orders = [tuple(reversed(o)) for o in axis_orders(dims)]
    total = 2 * NU
    rows = held.shape[-2]

    def remote(source, target, send, recv, device):
        return pltpu.make_async_remote_copy(
            src_ref=source, dst_ref=target, send_sem=send, recv_sem=recv, device_id=device, device_id_type=MESH
        )

    def unit(v):
        return 1 - v // NU, BACK[v % NU]

    def device_of(v, k):
        return other if k == 0 else partners[orders[v % SLOTS][k - 1]]

    def kept(v, k, sent):
        order = orders[v % SLOTS]
        where = []
        for i in range(dims):
            if i in order[: max(k - 1, 0)]:
                where.append(bits[i])
            elif k > 0 and i == order[k - 1]:
                where.append(1 - bits[i] if sent else bits[i])
            else:
                where.append(slice(None))
        return tuple(where)

    def load(v):
        layer, (matrix, block) = unit(v)
        source = part(grads[matrix], (layer,), (slice(None),) * dims, matrix, block, core)
        return pltpu.make_async_copy(source, held.at[v % SLOTS], load_sem.at[v % SLOTS])

    def step(v, k):
        slot = v % SLOTS
        if k == 0:
            layer, (matrix, block) = unit(v)
            source = part(grads[matrix], (layer,), (slice(None),) * dims, matrix, block, 1 - core)
        else:
            source = held.at[(slot,) + kept(v, k, True)]
        return remote(source, boxes[k].at[slot], send_sem.at[slot, k], recv_sem.at[slot, k], device_of(v, k))

    def start(v, k):
        if v >= SLOTS:
            pl.semaphore_wait(credit.at[v % SLOTS, k], 1)
        step(v, k).start()

    def add(v, k):
        slot = v % SLOTS
        where = kept(v, k, False)
        box = boxes[k].at[slot]
        view = held.at[(slot,) + where]
        if k < dims:
            view[...] = view[...] + box[...]
        else:
            total_sum = view[...].astype(jnp.float32) + box[...].astype(jnp.float32)
            result[slot] = total_sum
        if v + SLOTS < total:
            pl.semaphore_signal(credit.at[slot, k], inc=1, device_id=device_of(v, k), device_id_type=MESH)

    def final_place(v):
        layer, (matrix, block) = unit(v)
        return part(outs[matrix], (), (), matrix, block, core)

    def final_local(v):
        return pltpu.make_async_copy(result.at[v % SLOTS], final_place(v), out_sem.at[v % SLOTS])

    def final_remote(v):
        return remote(result.at[v % SLOTS], final_place(v), end_send.at[v % SLOTS], end_recv.at[v % NU], other)

    def finish(v, act):
        layer = unit(v)[0]
        if act == "start":

            @pl.when(core == layer)
            def _():
                final_local(v).start()

            @pl.when(core != layer)
            def _():
                final_remote(v).start()

        else:

            @pl.when(core == layer)
            def _():
                final_local(v).wait()

            @pl.when(core != layer)
            def _():
                final_remote(v).wait_send()

    small_first = remote(small.at[1 - core], small_box.at[0], small_send.at[0], small_recv.at[0], other)
    small_first.start()
    small_load = pltpu.make_async_copy(small.at[core], small_held, small_send.at[dims + 1])
    small_load.start()
    small_load.wait()
    small_first.wait()
    small_held[...] = small_held[...] + small_box[0]
    for k in range(1, dims + 1):
        i = k - 1
        lead = tuple(bits[:i])
        source = small_held.at[lead + (1 - bits[i],)]
        target = small_box.at[(k,) + lead + (bits[i],)]
        copy = remote(
            source, small_box.at[(k,) + lead + (1 - bits[i],)], small_send.at[k], small_recv.at[k], partners[i]
        )
        copy.start()
        copy.wait()
        mine = small_held.at[lead + (bits[i],)]
        mine[...] = mine[...] + target[...]
    out_copy = pltpu.make_async_copy(small_held.at[tuple(bits)], small_out, small_send.at[dims + 1])
    out_copy.start()
    out_copy.wait()

    for tick in range(total + dims + 2):
        for k in range(dims + 1, -1, -1):
            v = tick - k
            if not 0 <= v < total:
                continue
            if k == 0:
                if v >= SLOTS:
                    finish(v - SLOTS, "wait")
                load(v).start()
                start(v, 0)
            else:
                step(v, k - 1).wait()
                if k == 1:
                    load(v).wait()
                add(v, k - 1)
                if k <= dims:
                    start(v, k)
                else:
                    finish(v, "start")
    for v in range(total - SLOTS, total):
        finish(v, "wait")
    for layer in range(2):

        @pl.when(core == layer)
        def _():
            for v in range((1 - layer) * NU, (2 - layer) * NU):
                final_remote(v).wait_recv()


def scatter(grads, small, dims):
    rows = grads[1].shape[-2]
    shapes = [(rows, 3 * D), (rows, D), (rows, FF), (4, rows, D)]
    outs = [jax.ShapeDtypeStruct(s, jnp.float32) for s in shapes]
    outs.append(jax.ShapeDtypeStruct(small.shape[-2:], jnp.float32))
    dma = pltpu.SemaphoreType.DMA
    boxes = [pltpu.VMEM((SLOTS,) + (2,) * (dims - k) + (rows, HALF), jnp.bfloat16) for k in range(dims + 1)]
    return pl.pallas_call(
        functools.partial(scatter_kernel, dims),
        out_shape=outs,
        in_specs=[pl.BlockSpec(memory_space=pl.ANY)] * 5,
        out_specs=[pl.BlockSpec(memory_space=pl.ANY)] * 5,
        scratch_shapes=[pltpu.VMEM((SLOTS,) + (2,) * dims + (rows, HALF), jnp.bfloat16)]
        + boxes
        + [
            pltpu.VMEM((SLOTS, rows, HALF), jnp.float32),
            pltpu.VMEM(small.shape[1:], jnp.float32),
            pltpu.VMEM((dims + 1,) + small.shape[1:], jnp.float32),
            dma((SLOTS,)),
            dma((SLOTS, dims + 1)),
            dma((SLOTS, dims + 1)),
            pltpu.SemaphoreType.REGULAR((SLOTS, dims + 1)),
            dma((SLOTS,)),
            dma((SLOTS,)),
            dma((NU,)),
            dma((dims + 2,)),
            dma((dims + 1,)),
        ],
        compiler_params=pltpu.CompilerParams(collective_id=2, has_side_effects=True, vmem_limit_bytes=56 << 20),
        name="scatter",
    )(*grads, small)


def norm_parts(values):
    center = values - jnp.mean(values, -1, keepdims=True)
    factor = lax.rsqrt(jnp.mean(center * center, -1, keepdims=True) + EPS)
    return (center * factor, factor)


def norm_back(grad_normed, normed, factor):
    return factor * (
        grad_normed
        - jnp.mean(grad_normed, -1, keepdims=True)
        - normed * jnp.mean(grad_normed * normed, -1, keepdims=True)
    )


def gelu_exact(values):
    return jax.nn.gelu(values, approximate=False)


def forward(inputs, length, weights, is_last):
    w_qkv, w_out, w_up, w_down, vec_rows, up_bias = weights
    row_count = inputs.shape[0]
    positions = jnp.arange(row_count, dtype=jnp.int32)
    valid_rows = (positions < length).astype(jnp.float32)[:, None]
    allowed = (positions[None, :] <= positions[:, None]) & (positions[None, :] < length)
    normed_one, factor_one = norm_parts(inputs)
    attn_in = (normed_one * vec_rows[0] + vec_rows[1]).astype(jnp.bfloat16)
    projected = jnp.dot(attn_in, w_qkv, preferred_element_type=jnp.float32)
    query_heads = (projected[:, :D] + vec_rows[2]).astype(jnp.bfloat16).reshape(row_count, HEADS, HEAD_DIM)
    key_heads = projected[:, D : 2 * D].astype(jnp.bfloat16).reshape(row_count, HEADS, HEAD_DIM)
    value_heads = (projected[:, 2 * D :] + vec_rows[3]).astype(jnp.bfloat16).reshape(row_count, HEADS, HEAD_DIM)
    scores = jnp.einsum("qhd,khd->hqk", query_heads, key_heads, preferred_element_type=jnp.float32) * HEAD_DIM**-0.5
    scores = jnp.where(allowed[None], scores, -1e30)
    attn_probs = jax.nn.softmax(scores, axis=-1)
    probs_low = attn_probs.astype(jnp.bfloat16)
    attended = jnp.einsum("hqk,khd->qhd", probs_low, value_heads, preferred_element_type=jnp.float32)
    attended = attended.reshape(row_count, D).astype(jnp.bfloat16)
    hidden = inputs + jnp.dot(attended, w_out, preferred_element_type=jnp.float32) + vec_rows[4]
    normed_two, factor_two = norm_parts(hidden)
    ffn_in = (normed_two * vec_rows[5] + vec_rows[6]).astype(jnp.bfloat16)
    up_value = jnp.dot(ffn_in, w_up, preferred_element_type=jnp.float32) + up_bias
    activated = gelu_exact(up_value).astype(jnp.bfloat16)
    result = hidden + jnp.dot(activated, w_down, preferred_element_type=jnp.float32) + vec_rows[7]
    normed_three, factor_three = norm_parts(result)
    if is_last:
        result = normed_three * vec_rows[8] + vec_rows[9]
    result = result * valid_rows
    return result, (
        valid_rows,
        normed_one,
        factor_one,
        attn_in,
        query_heads,
        key_heads,
        value_heads,
        attn_probs,
        probs_low,
        attended,
        normed_two,
        factor_two,
        ffn_in,
        up_value,
        activated,
        normed_three,
        factor_three,
    )


def backward(saved, weights, is_last, cotangent):
    w_qkv, w_out, w_up, w_down, vec_rows, up_bias = weights
    (
        valid_rows,
        normed_one,
        factor_one,
        attn_in,
        query_heads,
        key_heads,
        value_heads,
        attn_probs,
        probs_low,
        attended,
        normed_two,
        factor_two,
        ffn_in,
        up_value,
        activated,
        normed_three,
        factor_three,
    ) = saved
    row_count = cotangent.shape[0]
    low = jnp.bfloat16
    grad_z = cotangent * valid_rows
    if is_last:
        grad_final_gain = jnp.sum(grad_z * normed_three, 0)
        grad_final_bias = jnp.sum(grad_z, 0)
        grad_y = norm_back(grad_z * vec_rows[8], normed_three, factor_three)
    else:
        grad_final_gain = jnp.zeros((D,), jnp.float32)
        grad_final_bias = jnp.zeros((D,), jnp.float32)
        grad_y = grad_z
    grad_branch = grad_y.astype(low)
    grad_down_bias = jnp.sum(grad_branch.astype(jnp.float32), 0)
    grad_down = jnp.einsum("sf,sd->fd", activated, grad_branch, preferred_element_type=jnp.float32).astype(low)
    grad_act = jnp.einsum("sd,fd->sf", grad_branch, w_down, preferred_element_type=jnp.float32)
    unused, gelu_pull = jax.vjp(gelu_exact, up_value)
    grad_upper = gelu_pull(grad_act)[0].astype(low)
    grad_upper_bias = jnp.sum(grad_upper.astype(jnp.float32), 0)
    grad_up = jnp.einsum("sd,sf->df", ffn_in, grad_upper, preferred_element_type=jnp.float32).astype(low)
    grad_ffn_in = jnp.einsum("sf,df->sd", grad_upper, w_up, preferred_element_type=jnp.float32)
    grad_gain_two = jnp.sum(grad_ffn_in * normed_two, 0)
    grad_bias_two = jnp.sum(grad_ffn_in, 0)
    grad_hidden = grad_y + norm_back(grad_ffn_in * vec_rows[5], normed_two, factor_two)
    grad_attn = grad_hidden.astype(low)
    grad_out_bias = jnp.sum(grad_attn.astype(jnp.float32), 0)
    grad_out = jnp.einsum("sa,sd->ad", attended, grad_attn, preferred_element_type=jnp.float32).astype(low)
    grad_mixed = jnp.einsum("sd,ad->sa", grad_attn, w_out, preferred_element_type=jnp.float32)
    grad_mixed = grad_mixed.astype(low).reshape(row_count, HEADS, HEAD_DIM)
    grad_probs = jnp.einsum("qhd,khd->hqk", grad_mixed, value_heads, preferred_element_type=jnp.float32)
    grad_value = jnp.einsum("hqk,qhd->khd", probs_low, grad_mixed, preferred_element_type=jnp.float32)
    grad_scores = attn_probs * (grad_probs - jnp.sum(grad_probs * attn_probs, -1, keepdims=True))
    grad_scores = grad_scores.astype(low)
    grad_query = jnp.einsum("hqk,khd->qhd", grad_scores, key_heads, preferred_element_type=jnp.float32) * HEAD_DIM**-0.5
    grad_key = jnp.einsum("hqk,qhd->khd", grad_scores, query_heads, preferred_element_type=jnp.float32) * HEAD_DIM**-0.5
    grad_proj = jnp.concatenate(
        [grad_query.reshape(row_count, D), grad_key.reshape(row_count, D), grad_value.reshape(row_count, D)], axis=1
    ).astype(low)
    grad_proj_wide = grad_proj.astype(jnp.float32)
    grad_query_bias = jnp.sum(grad_proj_wide[:, :D], 0)
    grad_value_bias = jnp.sum(grad_proj_wide[:, 2 * D :], 0)
    grad_qkv = jnp.einsum("sd,se->de", attn_in, grad_proj, preferred_element_type=jnp.float32).astype(low)
    grad_attn_in = jnp.einsum("se,de->sd", grad_proj, w_qkv, preferred_element_type=jnp.float32)
    grad_gain_one = jnp.sum(grad_attn_in * normed_one, 0)
    grad_bias_one = jnp.sum(grad_attn_in, 0)
    grad_inputs = grad_hidden + norm_back(grad_attn_in * vec_rows[0], normed_one, factor_one)
    grad_vec = jnp.stack(
        [
            grad_gain_one,
            grad_bias_one,
            grad_query_bias,
            grad_value_bias,
            grad_out_bias,
            grad_gain_two,
            grad_bias_two,
            grad_down_bias,
            grad_final_gain,
            grad_final_bias,
        ]
    )
    return (grad_inputs, (grad_qkv, grad_out, grad_up, grad_down, grad_vec, grad_upper_bias))


def small_layout(count):
    vec_lanes, bias_lanes = D // count, FF // count
    return vec_lanes, 128 // vec_lanes, bias_lanes, max(1, 128 // bias_lanes), max(1, bias_lanes // 128)


def pack_small(vectors, up_bias, count, here):
    vec_lanes, vec_group, bias_lanes, bias_group, bias_rows = small_layout(count)
    packed = jnp.zeros((16, 128), vectors.dtype)
    packed = lax.dynamic_update_slice(packed, vectors, (0, lax.rem(here, vec_group) * vec_lanes))
    wide = up_bias.reshape(bias_rows, bias_lanes // bias_rows)
    return lax.dynamic_update_slice(packed, wide, (10, lax.rem(here, bias_group) * bias_lanes if bias_group > 1 else 0))


def unpack_all(small, count):
    vec_lanes, vec_group, bias_lanes, bias_group, bias_rows = small_layout(count)
    small = small.reshape(2, count, 16, 128).astype(jnp.float32)
    vectors = small[:, :, :10].reshape(2, count // vec_group, vec_group, 10, 128).sum(2)
    vectors = vectors.transpose(0, 2, 1, 3).reshape(2, 10, D)
    bias = small[:, :, 10 : 10 + bias_rows].reshape(2, count // bias_group, bias_group, bias_rows * 128).sum(2)
    return vectors, bias.reshape(2, FF)


def pack_all(vectors, bias, count):
    vec_lanes, vec_group, bias_lanes, bias_group, bias_rows = small_layout(count)
    tiles = vectors.reshape(2, 10, D // 128, 128).transpose(0, 2, 1, 3)
    tiles = jnp.repeat(tiles, vec_group, axis=1)
    wide = jnp.repeat(bias.reshape(2, count // bias_group, bias_rows, 128), bias_group, axis=1)
    blank = jnp.zeros((2, count, 16 - 10 - bias_rows, 128), jnp.float32)
    return jnp.concatenate([tiles, wide, blank], axis=2)


def unpack_share(small, count, here):
    vec_lanes, vec_group, bias_lanes, bias_group, bias_rows = small_layout(count)
    vectors = lax.dynamic_slice(small, (0, lax.rem(here, vec_group) * vec_lanes), (10, vec_lanes))
    start = lax.rem(here, bias_group) * bias_lanes if bias_group > 1 else 0
    bias = lax.dynamic_slice(small, (10, start), (bias_rows, bias_lanes // bias_rows))
    return vectors, bias.reshape(bias_lanes)


def per_device(dims, hidden_in, lengths, out_grad, w_qkv, w_out, w_up, w_down, vectors, up_bias):
    core, here = lax.axis_index("pipe"), lax.axis_index("dp")
    count = 2**dims
    small = pack_small(vectors[0], up_bias[0], count, here)
    gathered = gather((w_qkv[0], w_out[0], w_up[0], w_down[0]), small, dims)
    qkv, out, up, down = (g.reshape(2, -1, g.shape[-1]) for g in gathered[:4])
    vec_rows, bias = unpack_all(gathered[4], count)
    weights = [(qkv[l], out[l], up[l], down[l], vec_rows[l], bias[l]) for l in range(2)]
    length = lax.dynamic_index_in_dim(lengths, core, 0, False)[0]
    states = lax.dynamic_index_in_dim(hidden_in, core, 0, False)[0].astype(jnp.float32)
    cotangent = lax.dynamic_index_in_dim(out_grad, core, 0, False)[0].astype(jnp.float32)
    first, saved_first = forward(states, length, weights[0], False)
    second_in = first.astype(jnp.bfloat16).astype(jnp.float32)
    result, saved_second = forward(second_in, length, weights[1], True)
    grad_second, grads_second = backward(saved_second, weights[1], True, cotangent)
    grad_first, grads_first = backward(
        saved_first, weights[0], False, grad_second.astype(jnp.bfloat16).astype(jnp.float32)
    )
    both = [jnp.stack([a, b]) for a, b in zip(grads_first, grads_second)]
    rows = D // count
    shards = [both[0], both[1], both[2], both[3]]
    shards = [s.reshape((2,) + (2,) * dims + (-1, s.shape[-1])) for s in shards[:3]] + [
        both[3].reshape((2,) + (2,) * dims + (4, rows, D))
    ]
    sums = scatter(shards, pack_all(both[4], both[5], count).reshape((2,) + (2,) * dims + (16, 128)), dims)
    grad_vec, grad_bias = unpack_share(sums[4], count, here)
    mine = jnp.where(core == 0, grad_first, result)
    theirs = lax.ppermute(jnp.where(core == 0, result, grad_first), "pipe", [(0, 1), (1, 0)])
    edges = jnp.where(core == 0, jnp.stack([mine, theirs]), jnp.stack([theirs, mine]))
    return (
        edges[None, :, None],
        sums[0][None],
        sums[1][None],
        sums[2][None],
        sums[3].reshape(1, -1, D),
        grad_vec[None],
        grad_bias[None],
    )


def solution(mesh):
    dims = (mesh.shape["dp"] - 1).bit_length()
    placed = (
        P(None, "dp", None, None),
        P(None, "dp"),
        P(None, "dp", None, None),
        P("pipe", "dp", None),
        P("pipe", "dp", None),
        P("pipe", "dp", None),
        P("pipe", "dp", None),
        P("pipe", None, "dp"),
        P("pipe", "dp"),
    )
    return jax.shard_map(
        functools.partial(per_device, dims),
        mesh=mesh,
        in_specs=placed,
        out_specs=(
            P("pipe", None, "dp", None, None),
            P("pipe", "dp", None),
            P("pipe", "dp", None),
            P("pipe", "dp", None),
            P("pipe", "dp", None),
            P("pipe", None, "dp"),
            P("pipe", "dp"),
        ),
        check_vma=False,
    )
```

time: 1950 us -> 894 us (0.46)
  waiting for transfers between devices: 1330 us -> 0.01 us
  Pallas kernels: 0 us -> 635 us
  blocking collectives: 156 us -> 0 us
  matrix products: 222 us -> 140 us
  other arithmetic: 124 us -> 47.6 us
    reduce_scatter x4 -> x0, waiting for transfers between devices: 928 us -> none  [the longest x1 355 us: per_device(): lax.psum_scatter(grads_now[3], 'dp', scatter_dimension=0, tiled=True)]
    pallas_call x0 -> x2, Pallas kernels: none -> 635 us  [the longest x1 329 us: gather(): pl.pallas_call(functools.partial(gather_kernel, dims), out_shape=outs, in...]
    all_gather x4 -> x0, waiting for transfers between devices: 302 us -> none  [the longest x1 114 us: per_device(): lax.all_gather(shards[2], 'dp', axis=1, tiled=True)]
    ppermute x4 -> x1, waiting for transfers between devices: 101 us -> 0.01 us  [per_device(): lax.ppermute(jnp.where(core == 0, result, grad_first), 'pipe', [(0, 1), (...]
    all_gather x2 -> x0, blocking collectives: 81.8 us -> none  [the longest x1 45.9 us: per_device(): lax.all_gather(shards[4], 'dp', axis=2, tiled=True)]
    add x12 -> x0, other arithmetic: 80.3 us -> none  [the longest x6 75.1 us: per_device(): running = tuple((total + term for total, term in zip(running, scattered)))]
    unnamed x1 -> x0, blocking collectives: 74.5 us -> none
    dot_general x22 -> x10, matrix products: 109 us -> 51.9 us  [the longest x2 32.9 us: forward(): jnp.dot(ffn_in, w_up, preferred_element_type=jnp.float32) + up_bias]
  transfers between devices with their start and end apart: 13 -> 1, of which waited for: 11 -> 0; matrix products, arithmetic and copies ran while one was open for 4% -> 8% of each run, Pallas kernels for 0% -> 34%
where the time goes in v1:
time: 894 us; the launch traced here: 890 us
  Pallas kernels  635 us (71%)
  matrix products  140 us (16%)
  local copies, waits for them, and re-layouts  65.3 us (7%)
  other arithmetic  47.6 us (5%)
    pallas_call x1, Pallas kernels, gather(): pl.pallas_call(functools.partial(gather_kernel, dims), out_shape=outs, in...  329 us
    pallas_call x1, Pallas kernels, scatter(): pl.pallas_call(functools.partial(scatter_kernel, dims), out_shape=outs, i...  306 us
    dot_general x2, matrix products, forward(): jnp.dot(ffn_in, w_up, preferred_element_type=jnp.float32) + up_bias  32.9 us
    another operation x5, other arithmetic, per_device(): both = [jnp.stack([a, b]) for a, b in zip(grads_first, grads_second)]  29.9 us
    dot_general x2, matrix products, backward(): jnp.einsum('sd,fd->sf', grad_branch, w_down, preferred_element_type=jnp.f...  23 us
  transfers between devices with their start and end apart: 1, of which 0 were waited for; matrix products, arithmetic and copies ran while one was open for 8% of the time, Pallas kernels for 34%

profile of v1, /device:TPU:0, one launch (start us, length us, event | category | flops | bytes accessed | tf_op | source)
XLA Modules:
  0.0 890.0 jit_solution(8489181054864065023)
XLA Ops:
  3.5 328.9 %gather.1 = (bf16[2,2,2,2,2,64,3072]{6,5,4,3,2,1,0:T(8,128)(2,1)}, bf16[2,2,2,2,2,64,1024]{6,5,4,3,2,1,0:T(8,128)(2,1)}, bf16[2,2,2,2,2,64,4096]{6,5,4,3,2,1,0:T...) custom-call(bf16[64,3072]{1,0:T(8,128)(2,1)} %bitcast.302, ...), custom_call_target="tpu_custom_call" | custom-call | tf_op jit(solution)/shard_map/gather/pallas_call | solution.py:163
  334.9 11.4 %fusion.139 = (bf16[1,2,2,2,2,64,3072]{6,5,4,3,2,1,0:T(8,128)(2,1)}, bf16[1,2,2,2,2,64,3072]{6,5,4,3,2,1,0:T(8,128)(2,1)}) fusion(bf16[2,2,2,2,2,64,3072]{6,5,4,3,2,1,0:T(8,128)(2,1)} %get-tuple-element.18), kind=kLoop, calls=%fused_computation.256 | loop fusion | bytes 25165824 | tf_op jit(solution)/shard_map/slice | solution.py:568
  348.1 4.7 fusion.87
  355.5 4.2 fusion.140
  359.7 12.5 %fusion.138 = (bf16[1,2,2,2,2,64,4096]{6,5,4,3,2,1,0:T(8,128)(2,1)}, bf16[1,2,2,2,2,64,4096]{6,5,4,3,2,1,0:T(8,128)(2,1)}) fusion(bf16[2,2,2,2,2,64,4096]{6,5,4,3,2,1,0:T(8,128)(2,1)} %get-tuple-element.20), kind=kLoop, calls=%fused_computation.255 | loop fusion | bytes 33554432 | tf_op jit(solution)/shard_map/slice | solution.py:568
  372.2 3.5 fusion.143
  375.7 2.9 convolution_convert_fusion.13
  379.7 10.6 %fusion.137 = (bf16[1,2,2,2,2,4,64,1024]{7,6,5,4,3,2,1,0:T(8,128)(2,1)}, bf16[1,2,2,2,2,4,64,1024]{7,6,5,4,3,2,1,0:T(8,128)(2,1)S(1)}) fusion(bf16[2,2,2,2,2,4,64,1024]{7,6,5,4,3,2,1,0:T(8,128)(2,1)} %get-tuple-element.21), kind=kLoop, calls=%fused_computation.254 | loop fusion | bytes 33554432 | tf_op jit(solution)/shard_map/slice | solution.py:568
  390.4 16.5 %multiply_convert_fusion.3 = (bf16[256,4096]{1,0:T(8,128)(2,1)S(1)}, f32[256,4096]{1,0:T(8,128)}, f32[256,4096]{1,0:T(8,128)}) fusion(f32[4096]{0:T(1024)S(1)} %bitcast.349, bf16[1024,4096]{1,0:T(8,128)(2,1)S(1)} %bitcast.225, f32[256,1024]{1,0:T(8,128)S(1)} %get-tuple-element.100, f32[1024]{0:T(1024)S(1)} %bitcast.314, f32[1024]{0:T(1024)S(1)} %bitcast.305, ...), kind=kOutput, calls=%fused_computation.41 | convolution fusion | flops 2218000384 | bytes 19949568 | tf_op jit(solution)/shard_map/dot_general | solution.py:411
  406.9 2.5 convert_reduce_fusion.2
  413.5 3.4 fusion.145
  417.0 2.9 convolution_convert_fusion.12
  422.5 16.4 %multiply_convert_fusion.2 = (bf16[256,4096]{1,0:T(8,128)(2,1)S(1)}, f32[256,4096]{1,0:T(8,128)}, f32[256,4096]{1,0:T(8,128)}) fusion(f32[4096]{0:T(1024)S(1)} %bitcast.348, bf16[1024,4096]{1,0:T(8,128)(2,1)S(1)} %bitcast.234, f32[256,1024]{1,0:T(8,128)S(1)} %get-tuple-element.107, f32[1024]{0:T(1024)S(1)} %bitcast.316, f32[1024]{0:T(1024)S(1)} %bitcast.309, ...), kind=kOutput, calls=%fused_computation.26 | convolution fusion | flops 2218000384 | bytes 19949568 | tf_op jit(solution)/shard_map/dot_general | solution.py:411
  438.9 2.4 fusion.147
  444.3 11.0 %convert_reduce_fusion = (f32[4096]{0:T(1024)S(1)}, bf16[256,4096]{1,0:T(8,128)(2,1)S(1)}) fusion(f32[256,4096]{1,0:T(8,128)S(1)} %copy-done.79, f32[256,4096]{1,0:T(8,128)} %get-tuple-element.108, bf16[4096,1024]{1,0:T(8,128)(2,1)} %bitcast.235, f32[256,1024]{1,0:T(8,128)S(1)} %get-tuple-element.56), kind=kOutput, calls=%fused_computation.18 | convolution fusion | flops 2164518912 | bytes 19939328 | tf_op jit(solution)/shard_map/sd,fd->sf/dot_general | solution.py:474
  455.4 6.9 multiply_reduce_fusion.2
  466.3 3.3 convolution_convert_fusion.10
  476.7 12.0 %convert_reduce_fusion.1 = (f32[4096]{0:T(1024)S(1)}, bf16[256,4096]{1,0:T(8,128)(2,1)S(1)}) fusion(f32[256,4096]{1,0:T(8,128)} %get-tuple-element.62, f32[256,4096]{1,0:T(8,128)} %get-tuple-element.101, bf16[4096,1024]{1,0:T(8,128)(2,1)} %bitcast.230, bf16[256,1024]{1,0:T(8,128)(2,1)S(1)} %get-tuple-element.52, f32[256]{0:T(256)S(1)} %get-tuple-element.124), kind=kOutput, calls=%fused_computation.19 | convolution fusion | flops 2165043200 | bytes 19416064 | tf_op jit(solution)/shard_map/sd,fd->sf/dot_general | solution.py:474
  488.8 2.7 multiply_reduce_fusion.3
  496.6 3.3 convolution_convert_fusion.8
  509.1 4.8 convolution_convert_fusion.4
  513.9 4.9 convolution_convert_fusion.5
  522.8 2.6 convolution_convert_fusion.2
  525.4 2.6 convolution_convert_fusion.3
  528.0 5.7 convolution_convert_fusion
  533.8 5.9 convolution_convert_fusion.1
  543.4 5.5 pad_maximum_fusion.2.refs_0_
  548.8 6.8 pad_maximum_fusion.refs_2_
  556.7 3.9 pad_maximum_fusion.3.refs_1_
  560.6 13.7 %pad_maximum_fusion.1.refs_3_ = bf16[2,2,2,2,2,4,64,1024]{7,6,5,4,3,2,1,0:T(8,128)(2,1)} fusion(bf16[1,2,2,2,2,4,64,1024]{7,6,5,4,3,2,1,0:T(8,128)(2,1)} %bitcast.213, bf16[1,2,2,2,2,4,64,1024]{7,6,5,4,3,2,1,0:T(8,128)(2,1)} %bitcast.214), kind=kLoop, calls=%fused_computation.3 | loop fusion | flops 8388608 | bytes 33554432 | tf_op jit(solution)/shard_map/stack | solution.py:579
  574.4 305.6 %scatter.1 = (f32[64,3072]{1,0:T(8,128)}, f32[64,1024]{1,0:T(8,128)}, f32[64,4096]{1,0:T(8,128)}, f32[4,64,1024]{2,1,0:T(8,128)}, f32[16,128]{1,0:T(8,128)}) custom-call(bf16[2,2,2,2,2,64,3072]{6,5,4,3,2,1,0:T(8,128)(2,1)} %pad_maximum_fusion.2.refs_0_, bf16[2,2,2,2,2,64,1024]{6,5,4,3,2,1,0:T(8,128)(2,1)} %pad_maximum_fusion.3.refs_1_, ...), custom_call_target="tpu_custom_call" | custom-call | tf_op jit(solution)/shard_map/scatter/pallas_call | solution.py:346
  882.8 3.5 maximum_select_fusion
  (298 shorter events, 60.4 us)
Async XLA Ops:
  0.6 345.7 %copy-start = (s32[2,1]{0,1:T(1,128)S(1)}, s32[2,1]{0,1:T(1,128)}, u32[]{:S(2)}) copy-start(s32[2,1]{0,1:T(1,128)} %param.10) | copy-start | bytes 28
  334.9 13.1 %copy-start.69 = (f32[1,1,8,128]{3,1,2,0:T(1,128)}, f32[1,1,8,128]{3,1,2,0:T(1,128)S(1)}, u32[]{:S(2)}) copy-start(f32[1,1,8,128]{3,1,2,0:T(1,128)S(1)} %get-tuple-element.94) | copy-start | bytes 12292
  334.9 13.2 %copy-start.77 = (f32[1,1,8,128]{3,1,2,0:T(1,128)}, f32[1,1,8,128]{3,1,2,0:T(1,128)S(1)}, u32[]{:S(2)}) copy-start(f32[1,1,8,128]{3,1,2,0:T(1,128)S(1)} %get-tuple-element.93) | copy-start | bytes 12292
  334.9 12.7 %copy-start.19 = (bf16[2,1,256,1024]{3,2,1,0:T(8,128)(2,1)S(1)}, bf16[2,1,256,1024]{3,2,1,0:T(8,128)(2,1)}, u32[]{:S(2)}) copy-start(bf16[2,1,256,1024]{3,2,1,0:T(8,128)(2,1)} %param.9) | copy-start | bytes 3145732
  354.5 17.7 %copy-start.46 = (bf16[256,1024]{0,1:T(8,128)(2,1)}, bf16[256,1024]{0,1:T(8,128)(2,1)S(1)}, u32[]{:S(2)}) copy-start(bf16[256,1024]{0,1:T(8,128)(2,1)S(1)} %copy.41) | copy-start | bytes 1572868
  359.7 18.9 %copy-start.2 = (bf16[1,2,2,2,2,64,1024]{6,5,4,3,2,1,0:T(8,128)(2,1)}, bf16[1,2,2,2,2,64,1024]{6,5,4,3,2,1,0:T(8,128)(2,1)S(1)}, u32[]{:S(2)}) copy-start(bf16[1,2,2,2,2,64,1024]{6,5,4,3,2,1,0:T(8,128)(2,1)S(1)} %get-tuple-element.72) | copy-start | bytes 6291460
  359.7 12.5 %copy-start.48 = (bf16[256,1024]{0,1:T(8,128)(2,1)S(1)}, bf16[256,1024]{0,1:T(8,128)(2,1)}, u32[]{:S(2)}) copy-start(bf16[256,1024]{0,1:T(8,128)(2,1)} %copy.42) | copy-start | bytes 1572868
  379.4 10.9 %slice-start = ((s8[8388608]{0:T(1024)(128)(4,1)}), s8[4194304]{0:T(1024)(128)(4,1)S(1)}, s32[]{:S(2)}) async-start(s8[8388608]{0:T(1024)(128)(4,1)} %bitcast.223), calls=%async_computation | async-start | bytes 8388608
  379.7 10.6 %slice-start.1 = ((s8[8388608]{0:T(1024)(128)(4,1)}), s8[4194304]{0:T(1024)(128)(4,1)S(1)}, s32[]{:S(2)}) async-start(s8[8388608]{0:T(1024)(128)(4,1)} %bitcast.223), calls=%async_computation.1 | async-start | bytes 8388608
  379.7 30.0 %slice-start.10 = ((s8[6291456]{0:T(1024)(128)(4,1)}), s8[4194304]{0:T(1024)(128)(4,1)S(1)}, s32[]{:S(2)}) async-start(s8[6291456]{0:T(1024)(128)(4,1)} %bitcast.243), calls=%async_computation.10 | async-start | bytes 8388608
  390.4 16.6 %copy-start.12 = (bf16[1,2,2,2,2,4,64,1024]{7,6,5,4,3,2,1,0:T(8,128)(2,1)}, bf16[1,2,2,2,2,4,64,1024]{7,6,5,4,3,2,1,0:T(8,128)(2,1)S(1)}, u32[]{:S(2)}) copy-start(bf16[1,2,2,2,2,4,64,1024]{7,6,5,4,3,2,1,0:T(8,128)(2,1)S(1)} %get-tuple-element.64) | copy-start | bytes 25165828
  390.4 19.4 %slice-start.11 = ((s8[6291456]{0:T(1024)(128)(4,1)}), s8[2097152]{0:T(1024)(128)(4,1)S(1)}, s32[]{:S(2)}) async-start(s8[6291456]{0:T(1024)(128)(4,1)} %bitcast.243), calls=%async_computation.11 | async-start | bytes 4194304
  409.4 10.4 %copy-start.13 = (bf16[256,1024]{1,0:T(8,128)(2,1)}, bf16[256,1024]{1,0:T(8,128)(2,1)S(1)}, u32[]{:S(2)}) copy-start(bf16[256,1024]{1,0:T(8,128)(2,1)S(1)} %get-tuple-element.103) | copy-start | bytes 1572868
  419.8 19.0 %copy-start.34 = (bf16[16,64,256]{2,1,0:T(8,128)(2,1)}, bf16[16,64,256]{2,1,0:T(8,128)(2,1)S(1)}, u32[]{:S(2)}) copy-start(bf16[16,64,256]{2,1,0:T(8,128)(2,1)S(1)} %convolution_convert_fusion.12) | copy-start | bytes 1572868
  419.9 19.0 %slice-start.6 = ((s8[8388608]{0:T(1024)(128)(4,1)}), s8[4194304]{0:T(1024)(128)(4,1)S(1)}, s32[]{:S(2)}) async-start(s8[8388608]{0:T(1024)(128)(4,1)} %bitcast.236), calls=%async_computation.6 | async-start | bytes 8388608
  422.5 16.4 %slice-start.7 = ((s8[8388608]{0:T(1024)(128)(4,1)}), s8[4194304]{0:T(1024)(128)(4,1)S(1)}, s32[]{:S(2)}) async-start(s8[8388608]{0:T(1024)(128)(4,1)} %bitcast.236), calls=%async_computation.7 | async-start | bytes 8388608
  441.4 14.0 %copy-start.7 = (f32[256,1024]{1,0:T(8,128)}, f32[256,1024]{1,0:T(8,128)S(1)}, u32[]{:S(2)}) copy-start(f32[256,1024]{1,0:T(8,128)S(1)} %get-tuple-element.110) | copy-start | bytes 3145732
  442.8 19.5 %copy-start.9 = (f32[256,1024]{1,0:T(8,128)}, f32[256,1024]{1,0:T(8,128)S(1)}, u32[]{:S(2)}) copy-start(f32[256,1024]{1,0:T(8,128)S(1)} %get-tuple-element.56) | copy-start | bytes 3145732
  474.0 14.8 %slice-start.2 = ((s8[8388608]{0:T(1024)(128)(4,1)}), s8[4194304]{0:T(1024)(128)(4,1)S(1)}, s32[]{:S(2)}) async-start(s8[8388608]{0:T(1024)(128)(4,1)} %bitcast.226), calls=%async_computation.2 | async-start | bytes 8388608
  476.6 14.9 %copy-start.16 = (bf16[256,1024]{1,0:T(8,128)(2,1)}, bf16[256,1024]{1,0:T(8,128)(2,1)S(1)}, u32[]{:S(2)}) copy-start(bf16[256,1024]{1,0:T(8,128)(2,1)S(1)} %get-tuple-element.52) | copy-start | bytes 1572868
  476.7 12.1 %slice-start.3 = ((s8[8388608]{0:T(1024)(128)(4,1)}), s8[4194304]{0:T(1024)(128)(4,1)S(1)}, s32[]{:S(2)}) async-start(s8[8388608]{0:T(1024)(128)(4,1)} %bitcast.226), calls=%async_computation.3 | async-start | bytes 8388608
  500.5 13.3 %copy-start.60 = (bf16[16,64,256]{2,1,0:T(8,128)(2,1)}, bf16[16,64,256]{2,1,0:T(8,128)(2,1)S(1)}, u32[]{:S(2)}) copy-start(bf16[16,64,256]{2,1,0:T(8,128)(2,1)S(1)} %convolution_convert_fusion.8) | copy-start | bytes 1572868
  503.7 10.1 %copy-start.42 = (bf16[16,64,256]{2,1,0:T(8,128)(2,1)}, bf16[16,64,256]{2,1,0:T(8,128)(2,1)S(1)}, u32[]{:S(2)}) copy-start(bf16[16,64,256]{2,1,0:T(8,128)(2,1)S(1)} %fusion.32) | copy-start | bytes 1572868
  504.2 9.6 %copy-start.44 = (bf16[16,64,256]{2,1,0:T(8,128)(2,1)}, bf16[16,64,256]{2,1,0:T(8,128)(2,1)S(1)}, u32[]{:S(2)}) copy-start(bf16[16,64,256]{2,1,0:T(8,128)(2,1)S(1)} %fusion.31) | copy-start | bytes 1572868
  508.7 374.1 %collective-permute-start = (f32[256,1024]{1,0:T(8,128)}, f32[256,1024]{1,0:T(8,128)}, u32[]{:S(2)}, u32[]{:S(2)}) collective-permute-start(f32[256,1024]{1,0:T(8,128)} %get-tuple-element.70), channel_id=1, source_target_pairs={{0,16},{16,0},{1,17},{17,1},{2,18},{18,2},{3,19},{19,3},{4,20},{20... | collective-permute-start | bytes 3145736 | tf_op jit(solution)/shard_map/ppermute | solution.py:588
  528.0 15.3 %slice-start.16 = ((s8[6291456]{0:T(1024)(128)(4,1)}), s8[2097152]{0:T(1024)(128)(4,1)S(1)}, s32[]{:S(2)}) async-start(s8[6291456]{0:T(1024)(128)(4,1)} %bitcast.252), calls=%async_computation.16 | async-start | bytes 4194304
  533.8 7.4 copy-start.45
  533.8 9.5 %slice-start.17 = ((s8[6291456]{0:T(1024)(128)(4,1)}), s8[4194304]{0:T(1024)(128)(4,1)S(1)}, s32[]{:S(2)}) async-start(s8[6291456]{0:T(1024)(128)(4,1)} %bitcast.252), calls=%async_computation.17 | async-start | bytes 8388608
  548.8 7.9 copy-start.11
  574.4 308.4 %copy-start.18 = (f32[1,1,1,256,1024]{4,3,2,1,0:T(8,128)S(1)}, f32[1,1,1,256,1024]{4,3,2,1,0:T(8,128)}, u32[]{:S(2)}) copy-start(f32[1,1,1,256,1024]{4,3,2,1,0:T(8,128)} %get-tuple-element.69) | copy-start | bytes 3145732
  880.0 7.2 copy-start.66
  880.0 7.9 copy-start.56
  (67 other events, 229.3 us)

commit v2 on v0

v2 whole, which is shorter than its diff:
```python
import functools
from types import SimpleNamespace

import jax
import jax.numpy as jnp
from jax import lax
from jax.experimental import pallas as pl
from jax.experimental.pallas import tpu as pltpu
from jax.sharding import PartitionSpec as P

D = 1024
HEADS = 16
HEAD_DIM = 64
FF = 4096
SEQ = 256
EPS = 1e-05
SCALE = HEAD_DIM**-0.5
MESH = pl.DeviceIdType.MESH
LOW = jnp.bfloat16
WIDE = jnp.float32
QKV, OUT, UP, DOWN = "qkv", "out", "up", "down"
FLAT = "_flat"
PIPE, DP = "pipe", "dp"
KINDS = [(QKV, 0), (QKV, 1), (QKV, 2), (OUT, 0), (UP, 0), (UP, 1), (DOWN, 0), (DOWN, 1)]
NU = len(KINDS)
GATHER_FIRST = -12
GATHER_LAGS = [2, 0, -3, -5]
GATHER_READY = 3
SMALL_AT = [0, 6, 12, 18, 24, 30]


def axis_order(dims, u):
    kind, block = KINDS[u]
    if kind in (UP, DOWN):
        return tuple(range(dims - 1))
    if dims == 4:
        return [(0, 1, 2, 3), (2, 0, 1, 3), (2, 0, 1, 3), (3, 0, 1, 2)][u]
    return tuple((i + 2 * u) % dims for i in range(dims))


def place(dims):
    core, here = lax.axis_index(PIPE), lax.axis_index(DP)
    bits = [lax.rem(lax.div(here, 2 ** (dims - 1 - i)), 2) for i in range(dims)]
    partners = [(core, here + (1 - 2 * bits[i]) * 2 ** (dims - 1 - i)) for i in range(dims)]
    return core, bits, partners, (1 - core, here)


def greet(everyone):
    barrier = pltpu.get_barrier_semaphore()
    for device in everyone:
        pl.semaphore_signal(barrier, inc=1, device_id=device, device_id_type=MESH)
    pl.semaphore_wait(barrier, len(everyone))


def remote(source, target, send, recv, device):
    return pltpu.make_async_remote_copy(
        src_ref=source, dst_ref=target, send_sem=send, recv_sem=recv, device_id=device, device_id_type=MESH
    )


def span(start, size):
    if isinstance(start, int):
        return pl.ds(start, size)
    return pl.ds(pl.multiple_of(start, size), size)


def for_each(count, body):
    lax.fori_loop(0, count, lambda i, carry: (body(i), carry)[1], 0)


def unit_columns(u, column_half):
    kind, block = KINDS[u]
    if kind == DOWN:
        return span(block * 512 + column_half * 256, 256)
    return span(block * 1024 + column_half * 512, 512)


def norm_parts(values):
    center = values - jnp.mean(values, -1, keepdims=True)
    factor = lax.rsqrt(jnp.mean(center * center, -1, keepdims=True) + EPS)
    return (center * factor, factor)


def norm_back(grad_normed, normed, factor):
    return factor * (
        grad_normed
        - jnp.mean(grad_normed, -1, keepdims=True)
        - normed * jnp.mean(grad_normed * normed, -1, keepdims=True)
    )


def dot(left, right, dims=((1,), (0,))):
    return lax.dot_general(left, right, (dims, ((), ())), preferred_element_type=WIDE)


BY_ROWS = ((0,), (0,))
BY_COLUMNS = ((1,), (1,))


def small_layout(count):
    vec_lanes, bias_lanes = D // count, FF // count
    return vec_lanes, 128 // vec_lanes, bias_lanes, max(1, 128 // bias_lanes), max(1, bias_lanes // 128)


def head_masks():
    lanes = lax.broadcasted_iota(jnp.int32, (1, 128), 1)
    first = (lanes < HEAD_DIM).astype(WIDE)
    return first, 1.0 - first


def valid_rows(length, start, count):
    rows = lax.broadcasted_iota(jnp.int32, (count, 1), 0) + start
    return (rows < length).astype(WIDE)


FORWARD_IN = ["w_qkv", "w_out", "w_up", "w_down", "small", "hidden", "lengths"]
S = "s_"
SAVED = ["x", "a", "q", "k", "v", "o", "p", "h", "c", "g", "gp"]
LOADS = ["vecs", "og", "y", "w_down", "w_up", "w_qkv", "w_out"] + SAVED
N = SimpleNamespace(**{n: n for n in LOADS})


def saved_shapes():
    wide = lambda *s: (s, WIDE)
    low = lambda *s: (s, LOW)
    return dict(
        x=low(SEQ, D),
        a=low(SEQ, D),
        q=low(SEQ, D),
        k=low(SEQ, D),
        v=low(SEQ, D),
        o=low(SEQ, D),
        p=low(HEADS, SEQ, SEQ),
        h=wide(SEQ, D),
        c=low(2, SEQ, D),
        g=low(2, SEQ, FF // 2),
        gp=low(2, SEQ, FF // 2),
    )


def forward_kernel(dims, names, *refs):
    R = SimpleNamespace(**dict(zip(names, refs)))
    core, bits, partners, sibling = place(dims)
    own = tuple(bits)
    half = bits[-1]
    mate = partners[-1]
    greet([sibling] + partners)
    total = 2 * NU
    count = 2**dims
    saved = SimpleNamespace(**{n: [getattr(R, n + str(l)) for l in range(2)] for n in SAVED})

    def first_pairs(u, layer, column_half):
        kind, block = KINDS[u]
        cols = unit_columns(u, column_half)
        if kind == UP:
            return [
                (R.w_up.at[half, :, cols], R.up.at[(layer,) + own + (slice(None), cols)]),
                (R.w_up.at[1 - half, :, cols], R.stage.at[layer, :, cols]),
            ]
        if kind == DOWN:
            return [(R.w_down.at[:, cols], R.down.at[(layer,) + own[:-1] + (slice(None), cols)])]
        return [(getattr(R, "w_" + kind).at[:, cols], getattr(R, kind).at[(layer,) + own + (slice(None), cols)])]

    def first_local(u, layer):
        return [
            pltpu.make_async_copy(s, t, R.local_sem.at[u, i])
            for i, (s, t) in enumerate(first_pairs(u, layer, core))
        ]

    def first_remote(u, layer):
        return [
            remote(s, t, R.first_send.at[u, i], R.first_recv.at[u, i], sibling)
            for i, (s, t) in enumerate(first_pairs(u, layer, 1 - core))
        ]

    def chain(v):
        layer, u = v // NU, v % NU
        kind, block = KINDS[u]
        cols = unit_columns(u, core)
        moves = []
        if kind == UP:
            moves.append((R.stage.at[layer, :, cols], R.up.at[(layer,) + own + (slice(None), cols)], mate))
        order = axis_order(dims, u)
        known = dims - 1 if kind == DOWN else dims
        free = {dims - 1} if kind == UP else set()
        for k in range(len(order) + 1):
            gathered = set(order[:k]) | free
            where = tuple(slice(None) if i in gathered else bits[i] for i in range(known))
            ref = getattr(R, kind).at[(layer,) + where + (slice(None), cols)]
            moves.append((ref, ref, partners[order[k]] if k < len(order) else sibling))
        return [remote(s, t, R.send.at[v, i], R.recv.at[v, i], d) for i, (s, t, d) in enumerate(moves)]

    def small_step(k):
        where = tuple(slice(None) if i < k else bits[i] for i in range(dims))
        ref = R.small_all.at[(core,) + where]
        return remote(ref, ref, R.small_send.at[k], R.small_recv.at[k], partners[k] if k < dims else sibling)

    small_own = pltpu.make_async_copy(R.small, R.small_all.at[(core,) + own], R.io.at[0])
    small_own.start()
    load_x = pltpu.make_async_copy(R.hidden.at[core], saved.x[0], R.io.at[1])
    load_x.start()
    for layer in range(2):

        @pl.when(core == layer)
        def _():
            for u in range(NU):
                for copy in first_remote(u, layer) + first_local(u, layer):
                    copy.start()

    def arrive(v):
        layer, u = v // NU, v % NU

        @pl.when(core == layer)
        def _():
            for copy in first_local(u, layer):
                copy.wait()
            for copy in first_remote(u, layer):
                copy.wait_send()

        @pl.when(core != layer)
        def _():
            for copy in first_remote(u, layer):
                copy.wait_recv()

    length = R.lengths[core]
    vecs, biases = R.vecs, R.biases
    first_head, second_head = head_masks()

    def assemble():
        vec_lanes, vec_group, bias_lanes, bias_group, bias_rows = small_layout(count)
        small = R.small_all

        def shard(layer, d):
            return small[(layer,) + tuple((d >> (dims - 1 - i)) & 1 for i in range(dims))].astype(WIDE)

        def half_shard(layer, b):
            lead = tuple((b >> (dims - 2 - i)) & 1 for i in range(dims - 1))
            return small[(layer,) + lead + (half,)].astype(WIDE)

        for layer in range(2):
            for t in range(D // 128):
                vecs[layer, :, t * 128 : (t + 1) * 128] = sum(
                    shard(layer, d) for d in range(t * vec_group, (t + 1) * vec_group)
                )
            for t in range(count // 2 // bias_group):
                tile = sum(half_shard(layer, b) for b in range(t * bias_group, (t + 1) * bias_group))
                for i in range(bias_rows):
                    at = (t * bias_rows + i) * 128
                    biases[layer, 0:1, at : at + 128] = tile[10 + i : 11 + i, :]

    save_queue = []

    def save(name, layer):
        copy = pltpu.make_async_copy(
            getattr(saved, name)[layer], getattr(R, S + name).at[layer], R.save_sem.at[layer, SAVED.index(name)]
        )
        copy.start()
        save_queue.append(copy)

    def vec(layer, i, cols=slice(None)):
        return vecs[layer, i : i + 1, cols]

    def load_weight(v):
        layer, u = v // NU, v % NU
        kind, block = KINDS[u]
        if kind == DOWN:
            flat = R.down_flat.at[layer, :, pl.ds(block * 512, 512)]
            target = R.w_low.at[:, pl.ds(block * 512, 512)]
        else:
            flat = getattr(R, kind + FLAT).at[layer, :, pl.ds(block * 1024, 1024)]
            target = R.w_slots.at[u % 2]
        return pltpu.make_async_copy(flat, target, R.weight_sem.at[u % 4])

    def first_norm(layer):
        def rows(i):
            at = span(i * 32, 32)
            normed, unused = norm_parts(saved.x[layer][at, :].astype(WIDE))
            saved.a[layer][at, :] = (normed * vec(layer, 0) + vec(layer, 1)).astype(LOW)

        for_each(SEQ // 32, rows)
        save(N.x, layer)
        save(N.a, layer)

    def project(layer, block):
        target = (saved.q, saved.k, saved.v)[block][layer]
        weight = R.w_slots.at[block % 2]

        def columns(n):
            at = span(n * 256, 256)
            values = dot(saved.a[layer][...], weight[:, at])
            if block == 0:
                values = (values + vec(layer, 2, at)).astype(LOW) * SCALE
            elif block == 2:
                values = values + vec(layer, 3, at)
            target[:, at] = values.astype(LOW)

        for_each(D // 256, columns)
        save((N.q, N.k, N.v)[block], layer)

    def attention(layer):
        key_ids = lax.broadcasted_iota(jnp.int32, (SEQ, SEQ), 0)
        query_ids = lax.broadcasted_iota(jnp.int32, (SEQ, SEQ), 1)
        blocked = jnp.where((key_ids <= query_ids) & (key_ids < length), 0.0, -1e30)

        def pair(n):
            at = span(n * 128, 128)
            query, key, value = (part[layer][:, at] for part in (saved.q, saved.k, saved.v))
            parts = []
            for i, mask in enumerate((first_head, second_head)):
                scores = dot(key, query * mask.astype(LOW), BY_COLUMNS) + blocked
                weights = jnp.exp(scores - jnp.max(scores, 0, keepdims=True))
                probs = (weights * (1.0 / jnp.sum(weights, 0, keepdims=True))).astype(LOW)
                saved.p[layer][2 * n + i] = probs
                parts.append(dot(probs, value, BY_ROWS) * mask)
            saved.o[layer][:, at] = (parts[0] + parts[1]).astype(LOW)

        for_each(HEADS // 2, pair)
        save(N.p, layer)
        save(N.o, layer)

    def send_c(layer):
        ref = saved.c[layer]
        return remote(ref.at[0], ref.at[1], R.act_send.at[layer, 0], R.act_recv.at[layer, 0], mate)

    def attend_out(layer):
        weight = R.w_slots.at[1]
        hidden = saved.h[layer]

        def columns(n):
            at = span(n * 256, 256)
            values = dot(saved.o[layer][...], weight[:, at])
            hidden[:, at] = saved.x[layer][:, at].astype(WIDE) + values + vec(layer, 4, at)

        def rows(i):
            at = span(i * 32, 32)
            normed, unused = norm_parts(hidden[at, :])
            saved.c[layer][0, at, :] = (normed * vec(layer, 5) + vec(layer, 6)).astype(LOW)

        for_each(D // 256, columns)
        for_each(SEQ // 32, rows)
        send_c(layer).start()
        save(N.h, layer)

    def feed_up(layer, block):
        if block == 0:
            send_c(layer).wait()
            save(N.c, layer)
        weight = R.w_slots.at[block]

        def columns(n):
            at = span(n * 256, 256)
            to = span(block * 1024 + n * 256, 256)
            for who in range(2):
                value = dot(saved.c[layer][who], weight[:, at]) + biases[layer, 0:1, to]
                share = 0.5 + 0.5 * lax.erf(value * 0.7071067811865476)
                slope = share + value * (jnp.exp(value * value * -0.5) * 0.3989422804014327)
                saved.g[layer][who, :, to] = (value * share).astype(LOW)
                saved.gp[layer][who, :, to] = slope.astype(LOW)

        for_each(4, columns)
        if block == 1:
            save(N.g, layer)
            save(N.gp, layer)

    def send_part(layer, block):
        at = pl.ds(block * 512, 512)
        return remote(
            R.part.at[layer, 0, :, at],
            R.part.at[layer, 1, :, at],
            R.act_send.at[layer, 1 + block],
            R.act_recv.at[layer, 1 + block],
            mate,
        )

    def feed_down(layer, block):
        def theirs(n):
            at = span(block * 512 + n * 256, 256)
            R.part[layer, 0, :, at] = dot(saved.g[layer][1], R.w_low[:, at]).astype(LOW)

        def mine(n):
            at = span(block * 512 + n * 256, 256)
            values = dot(saved.g[layer][0], R.w_low[:, at])
            R.y[:, at] = saved.h[layer][:, at] + values + vec(layer, 7, at)

        for_each(2, theirs)
        send_part(layer, block).start()
        for_each(2, mine)

    def end(layer):
        for block in range(2):
            send_part(layer, block).wait()

        def rows(i):
            at = span(i * 32, 32)
            valid = valid_rows(length, i * 32, 32)
            values = R.y[at, :] + R.part[layer, 1, at, :].astype(WIDE)
            if layer == 0:
                saved.x[1][at, :] = (values * valid).astype(LOW)
            else:
                R.y[at, :] = values
                normed, unused = norm_parts(values)
                R.z[at, :] = (normed * vec(1, 8) + vec(1, 9)) * valid

        for_each(SEQ // 32, rows)

    def work(v):
        layer, u = v // NU, v % NU
        kind, block = KINDS[u]
        load_weight(v).start()
        if u == 0:
            first_norm(layer)
        load_weight(v).wait()
        if kind == QKV:
            project(layer, block)
            if block == 2:
                attention(layer)
        elif kind == OUT:
            attend_out(layer)
        elif kind == UP:
            feed_up(layer, block)
        else:
            feed_down(layer, block)
            if block == 1:
                end(layer)

    chains = [chain(v) for v in range(total)]
    events = []
    for v in range(total):
        for i in range(len(chains[v])):
            left = len(chains[v]) - 1 - i
            lag = GATHER_LAGS[left] if left < len(GATHER_LAGS) else GATHER_LAGS[-1] - left + len(GATHER_LAGS) - 1
            events.append((v + (lag if i else min(GATHER_FIRST, lag)), -i, v))
        events.append((v + GATHER_READY, -9, v))
    events = [(v, -i) for unused, i, v in sorted(events)]
    for k in range(dims + 2):
        events.insert(SMALL_AT[min(k, len(SMALL_AT) - 1)] + max(0, k - 5), (-1, k))
    small_own.wait()
    load_x.wait()
    for v, i in events:
        if v < 0:
            if i > 0:
                small_step(i - 1).wait()
            if i <= dims:
                small_step(i).start()
            else:
                assemble()
        elif i == 9:
            chains[v][-1].wait()
            work(v)
        else:
            if i == 0:
                arrive(v)
            else:
                chains[v][i - 1].wait()
            chains[v][i].start()

    last = [(R.y, R.s_y, 0), (R.z, R.s_z, 1), (R.vecs, R.s_vecs, 2)]
    for source, target, i in last:
        pltpu.make_async_copy(source, target, R.last_sem.at[i]).start()
    for copy in save_queue:
        copy.wait()
    for source, target, i in last:
        pltpu.make_async_copy(source, target, R.last_sem.at[i]).wait()


def forward(shards, small, hidden, lengths, dims):
    rows = D // 2**dims
    bits = (2,) * dims
    outs = dict(
        qkv=((2,) + bits + (rows, 3 * D), LOW),
        out=((2,) + bits + (rows, D), LOW),
        up=((2,) + bits + (rows, FF // 2), LOW),
        down=((2,) + bits[:-1] + (4 * rows, D), LOW),
        stage=((2, rows, FF // 2), LOW),
    )
    for name, (shape, dtype) in saved_shapes().items():
        outs[S + name] = ((2,) + shape, dtype)
    outs[S + N.y] = ((SEQ, D), WIDE)
    outs[S + "z"] = ((SEQ, D), WIDE)
    outs[S + N.vecs] = ((2, 16, D), WIDE)
    dma = pltpu.SemaphoreType.DMA
    total = 2 * NU
    scratch = dict(
        small_all=pltpu.VMEM((2,) + bits + (16, 128), LOW),
        vecs=pltpu.VMEM((2, 16, D), WIDE),
        biases=pltpu.VMEM((2, 8, FF // 2), WIDE),
        w_slots=pltpu.VMEM((2, D, D), LOW),
        w_low=pltpu.VMEM((FF // 2, D), LOW),
        part=pltpu.VMEM((2, 2, SEQ, D), LOW),
        y=pltpu.VMEM((SEQ, D), WIDE),
        z=pltpu.VMEM((SEQ, D), WIDE),
        local_sem=dma((NU, 2)),
        first_send=dma((NU, 2)),
        first_recv=dma((NU, 2)),
        send=dma((total, dims + 2)),
        recv=dma((total, dims + 2)),
        small_send=dma((dims + 1,)),
        small_recv=dma((dims + 1,)),
        io=dma((2,)),
        save_sem=dma((2, len(SAVED))),
        weight_sem=dma((4,)),
        act_send=dma((2, 3)),
        act_recv=dma((2, 3)),
        last_sem=dma((3,)),
    )
    for name, (shape, dtype) in saved_shapes().items():
        for layer in range(2):
            scratch[name + str(layer)] = pltpu.VMEM(shape, dtype)
    names = FORWARD_IN + list(outs) + list(scratch)

    def kernel(*refs):
        by_name = dict(zip(names, refs))
        extra = dict(
            qkv_flat=by_name[QKV].reshape(2, D, 3 * D),
            out_flat=by_name[OUT].reshape(2, D, D),
            up_flat=by_name[UP].reshape(2, D, FF // 2),
            down_flat=by_name[DOWN].reshape(2, FF // 2, D),
        )
        forward_kernel(dims, names + list(extra), *refs, *extra.values())

    anywhere = pl.BlockSpec(memory_space=pl.ANY)
    results = pl.pallas_call(
        kernel,
        out_shape=[jax.ShapeDtypeStruct(s, t) for s, t in outs.values()],
        in_specs=[anywhere] * 6 + [pl.BlockSpec(memory_space=pltpu.SMEM)],
        out_specs=[anywhere] * len(outs),
        scratch_shapes=list(scratch.values()),
        compiler_params=pltpu.CompilerParams(collective_id=1, has_side_effects=True, vmem_limit_bytes=60 << 20),
        name="forward",
    )(*shards, small, hidden, lengths)
    return dict(zip(outs, results))


def pack_small(vectors, up_bias, count, here):
    vec_lanes, vec_group, bias_lanes, bias_group, bias_rows = small_layout(count)
    packed = jnp.zeros((16, 128), vectors.dtype)
    packed = lax.dynamic_update_slice(packed, vectors, (0, lax.rem(here, vec_group) * vec_lanes))
    wide = up_bias.reshape(bias_rows, bias_lanes // bias_rows)
    at = lax.rem(lax.div(here, 2), bias_group) * bias_lanes if bias_group > 1 else 0
    return lax.dynamic_update_slice(packed, wide, (10, at))


def forward_call(dims, here, core, hidden_in, lengths, w_qkv, w_out, w_up, w_down, vectors, up_bias):
    count = 2**dims
    rows = D // count
    small = pack_small(vectors[0], up_bias[0], count, here)
    halves = w_up[0].reshape(rows, count // 2, 2, FF // count).transpose(2, 0, 1, 3).reshape(2, rows, FF // 2)
    return forward((w_qkv[0], w_out[0], halves, w_down[0]), small, hidden_in[:, 0], lengths[:, 0], dims)
BACK = [(DOWN, 0), (DOWN, 1), (UP, 0), (UP, 1), (OUT, 0), (QKV, 0), (QKV, 1), (QKV, 2)]
SCATTER_LAGS = [1, 3, 4, 5, 6]
HELD, B = "held", "b_"
BACK_WEIGHTS = [QKV, OUT, UP, DOWN]
BACK_IN = BACK_WEIGHTS + [S + n for n in SAVED + ["y", "z", "vecs"]] + ["out_grad", "lengths"]


def box_name(u, k):
    return "box%d_%d" % (u, k)


def backward_kernel(dims, names, *refs):
    R = SimpleNamespace(**dict(zip(names, refs)))
    core, bits, partners, sibling = place(dims)
    own = tuple(bits)
    half = bits[-1]
    mate = partners[-1]
    greet([sibling] + partners)
    total = 2 * NU
    count = 2**dims
    length = R.lengths[core]
    vecs, grads = R.vecs, R.grads
    first_head, second_head = head_masks()

    def load(name, layer):
        if name == N.y:
            source = R.s_y
        elif name == N.og:
            source = R.out_grad.at[core]
        elif name == N.vecs:
            source = R.s_vecs
        elif name in (N.w_down, N.w_up, N.w_qkv, N.w_out):
            source = getattr(R, name[2:] + FLAT).at[layer]
        else:
            source = getattr(R, S + name).at[layer]
        if name == N.vecs:
            target = vecs
        elif name == N.w_up:
            target = R.b_w_wide.at[:, pl.ds(0, FF // 2)]
        elif name == N.w_qkv:
            target = R.b_w_wide
        else:
            target = getattr(R, B + name)
        return pltpu.make_async_copy(source, target, R.load_sem.at[LOADS.index(name)])

    def need(layer, *which):
        for name in which:
            load(name, layer).wait()

    def again(layer, *which):
        if layer == 1:
            for name in which:
                load(name, 0).start()

    def unit_of(v):
        return 1 - v // NU, BACK[v % NU]

    def columns_of(v, column_half):
        kind, block = BACK[v % NU]
        if kind == DOWN:
            return span(block * 512 + column_half * 256, 256)
        return span(block * 1024 + column_half * 512, 512)

    def order_of(v):
        return tuple(reversed(axis_order(dims, KINDS.index(BACK[v % NU]))))

    def held(v):
        return getattr(R, HELD + str(v % NU))

    def box(v, k):
        if k == 0:
            kind, block = BACK[v % NU]
            return (R.down_box if kind == DOWN else R.wide_box).at[v % 2]
        return getattr(R, box_name(v % NU, k))

    def stage(v):
        kind, block = BACK[v % NU]
        return (R.down_stage if kind == DOWN else R.wide_stage).at[v % 2]

    def is_up(v):
        return BACK[v % NU][0] == UP

    def steps(v):
        return len(order_of(v)) + (1 if is_up(v) else 0)

    def where(v, k, away):
        order = order_of(v)
        place_of = []
        for i in range(dims - 1 if BACK[v % NU][0] == DOWN else dims):
            if i in order[: max(k - 1, 0)]:
                place_of.append(bits[i])
            elif 0 < k <= len(order) and i == order[k - 1]:
                place_of.append(1 - bits[i] if away else bits[i])
            elif k > len(order) and i == dims - 1:
                place_of.append(1 - half if away else half)
            elif k > len(order):
                place_of.append(bits[i])
            else:
                place_of.append(slice(None))
        return tuple(place_of)

    def device_of(v, k):
        if k == 0:
            return sibling
        return partners[order_of(v)[k - 1]] if k <= len(order_of(v)) else mate

    def move(v, k):
        source = stage(v) if k == 0 else held(v).at[where(v, k, True)]
        return remote(source, box(v, k), R.send.at[v, k], R.recv.at[v, k], device_of(v, k))

    def earlier(v, k):
        if k > 0 or BACK[v % NU][0] == DOWN:
            return v - NU if v >= NU else None
        wide = [w for w in range(total) if BACK[w % NU][0] != DOWN and w % 2 == v % 2 and w < v]
        return wide[-1] if wide else None

    def later(v, k):
        return any(earlier(w, k) == v for w in range(v + 1, total))

    def begin(v, k):
        if earlier(v, k) is not None:
            pl.semaphore_wait(R.credit.at[v % NU, k], 1)
        move(v, k).start()

    def consumed(v, k):
        for w in range(v + 1, total):
            if earlier(w, k) == v:
                pl.semaphore_signal(
                    R.credit.at[w % NU, k], inc=1, device_id=device_of(v, k), device_id_type=MESH
                )

    def finals(v):
        kind, block = BACK[v % NU]
        cols = columns_of(v, core)
        if kind == UP:
            return [
                (held(v).at[own], R.g_up.at[half, :, cols]),
                (box(v, dims), R.g_up.at[1 - half, :, cols]),
            ]
        if kind == DOWN:
            return [(held(v).at[own[:-1]], R.g_down.at[:, cols])]
        return [(held(v).at[own], getattr(R, "g_" + kind).at[:, cols])]

    def final_local(v):
        return [
            pltpu.make_async_copy(s, t, R.out_sem.at[v, i]) for i, (s, t) in enumerate(finals(v))
        ]

    def final_remote(v):
        return [
            remote(s, t, R.end_send.at[v, i], R.end_recv.at[v, i], sibling)
            for i, (s, t) in enumerate(finals(v))
        ]

    def finish(v):
        @pl.when(core == unit_of(v)[0])
        def _():
            for copy in final_local(v):
                copy.start()

        @pl.when(core != unit_of(v)[0])
        def _():
            for copy in final_remote(v):
                copy.start()

    def finished(v):
        @pl.when(core == unit_of(v)[0])
        def _():
            for copy in final_local(v):
                copy.wait()

        @pl.when(core != unit_of(v)[0])
        def _():
            for copy in final_remote(v):
                copy.wait_send()
        if is_up(v):
            consumed(v, dims)

    def event(v, k):
        move(v, k).wait()
        if not (is_up(v) and k == steps(v)):
            view = held(v).at[where(v, k, False)]
            view[...] = view[...] + box(v, k)[...]
            consumed(v, k)
        if k < steps(v):
            begin(v, k + 1)
        else:
            finish(v)

    def vec(layer, i):
        return vecs[layer, i : i + 1, :]

    def collect(layer, i, values):
        grads[layer, i : i + 1, :] = grads[layer, i : i + 1, :] + jnp.sum(values, 0, keepdims=True)

    def send_e(layer):
        ref = R.e
        return remote(ref.at[0], ref.at[1], R.act_send.at[layer, 0], R.act_recv.at[layer, 0], mate)

    def send_dc(layer):
        ref = R.dc_part
        return remote(ref.at[0], ref.at[1], R.act_send.at[layer, 1], R.act_recv.at[layer, 1], mate)

    def top(layer):
        if layer == 1:
            need(1, N.vecs, N.og, N.y)

        def rows(i):
            at = span(i * 32, 32)
            valid = valid_rows(length, i * 32, 32)
            if layer == 1:
                grad_z = R.b_og[at, :].astype(WIDE) * valid
                normed, factor = norm_parts(R.b_y[at, :])
                collect(1, 8, grad_z * normed)
                collect(1, 9, grad_z)
                grad_y = norm_back(grad_z * vec(1, 8), normed, factor)
            else:
                grad_y = R.dx[at, :].astype(WIDE) * valid
            R.dy[at, :] = grad_y
            branch = grad_y.astype(LOW)
            R.e[0, at, :] = branch
            collect(layer, 7, branch.astype(WIDE))

        for_each(SEQ // 32, rows)
        send_e(layer).start()

    def produce(v, body, quarter_shape):
        for target, column_half in ((stage(v), 1 - core), (held(v), core)):
            cols = columns_of(v, column_half)

            def quarter(i):
                target[lax.div(i, 2), lax.rem(i, 2)] = body(i, cols).astype(LOW).reshape(quarter_shape)

            for_each(4, quarter)
            if column_half is not core:
                begin(v, 0)

    def pair_rows(ref, cols):
        values = ref[:, :, cols]
        return values.reshape(2 * SEQ, values.shape[-1])

    inner = (2,) * (dims - 2) + (D // count, 512)
    down_inner = (2,) * (dims - 3) + (FF // count, 256)

    def grad_down(layer, v, block):
        if block == 0:
            need(layer, N.g)
            send_e(layer).wait()
        produce(
            v,
            lambda i, cols: dot(pair_rows(R.b_g, span(i * 512, 512)), pair_rows(R.e, cols), BY_ROWS),
            down_inner,
        )
        if block == 1:
            again(layer, N.g)

    def feed_back(layer):
        need(layer, N.w_down, N.gp)

        def hidden(n):
            at = span(n * 256, 256)
            rows = pair_rows(R.e, slice(None))
            grad_act = dot(rows, R.b_w_down[at, :], BY_COLUMNS)
            grad_upper = (grad_act * pair_rows(R.b_gp, at).astype(WIDE)).astype(LOW)
            R.b_gp[:, :, at] = grad_upper.reshape(2, SEQ, 256)
            R.bias_grads[layer, 0:1, at] = jnp.sum(grad_upper.astype(WIDE), 0, keepdims=True)

        for_each(FF // 2 // 256, hidden)
        again(layer, N.w_down)
        need(layer, N.w_up)
        wide = pl.ds(0, FF // 2)

        def theirs(n):
            at = span(n * 256, 256)
            R.dc_part[0, :, at] = dot(R.b_gp[1], R.b_w_wide[at, wide], BY_COLUMNS).astype(LOW)

        def mine(n):
            at = span(n * 256, 256)
            R.dc[:, at] = dot(R.b_gp[0], R.b_w_wide[at, wide], BY_COLUMNS)

        for_each(D // 256, theirs)
        send_dc(layer).start()
        for_each(D // 256, mine)
        load(N.w_qkv, layer).start()

    def grad_up(layer, v, block):
        if block == 0:
            need(layer, N.c)

        def body(i, cols):
            return dot(pair_rows(R.b_c, span(i * 256, 256)), pair_rows(R.b_gp, cols), BY_ROWS)

        produce(v, body, inner)
        if block == 1:
            again(layer, N.c, N.gp)

    def middle(layer):
        need(layer, N.h)
        send_dc(layer).wait()

        def rows(i):
            at = span(i * 32, 32)
            grad_in = R.dc[at, :] + R.dc_part[1, at, :].astype(WIDE)
            normed, factor = norm_parts(R.b_h[at, :])
            collect(layer, 5, grad_in * normed)
            collect(layer, 6, grad_in)
            grad_hidden = R.dy[at, :] + norm_back(grad_in * vec(layer, 5), normed, factor)
            R.dy[at, :] = grad_hidden
            branch = grad_hidden.astype(LOW)
            R.f[at, :] = branch
            collect(layer, 4, branch.astype(WIDE))

        for_each(SEQ // 32, rows)
        again(layer, N.h)

    def grad_out(layer, v):
        need(layer, N.o)
        produce(v, lambda i, cols: dot(R.b_o[:, span(i * 256, 256)], R.f[:, cols], BY_ROWS), inner)
        again(layer, N.o)

    def attention_back(layer):
        need(layer, N.w_out)

        def columns(n):
            at = span(n * 256, 256)
            R.do[:, at] = dot(R.f[...], R.b_w_out[at, :], BY_COLUMNS).astype(LOW)

        for_each(D // 256, columns)
        again(layer, N.w_out)
        need(layer, N.q, N.k, N.v, N.p)

        def pair(n):
            at = span(n * 128, 128)
            query, key, value, grad_o = R.b_q[:, at], R.b_k[:, at], R.b_v[:, at], R.do[:, at]
            sums = [0.0, 0.0, 0.0]
            for i, mask in enumerate((first_head.astype(LOW), second_head.astype(LOW))):
                probs = R.b_p[2 * n + i]
                grad_head = grad_o * mask
                wide = probs.astype(WIDE)
                grad_probs = dot(value, grad_head, BY_COLUMNS)
                shift = jnp.sum(grad_probs * wide, 0, keepdims=True)
                grad_scores = (wide * (grad_probs - shift)).astype(LOW)
                sums[0] += dot(grad_scores, key * mask, BY_ROWS)
                sums[1] += dot(grad_scores, query * mask)
                sums[2] += dot(probs, grad_head)
            sums[0] = sums[0] * SCALE
            for j in range(3):
                low = sums[j].astype(LOW)
                R.dp[:, pl.ds(pl.multiple_of(n * 128 + j * D, 128), 128)] = low
                if j != 1:
                    row = 2 if j == 0 else 3
                    grads[layer, row : row + 1, at] = jnp.sum(low.astype(WIDE), 0, keepdims=True)

        for_each(HEADS // 2, pair)
        again(layer, N.q, N.k, N.v, N.p)

    def grad_qkv(layer, v, block):
        if block == 0:
            need(layer, N.a)
        produce(v, lambda i, cols: dot(R.b_a[:, span(i * 256, 256)], R.dp[:, cols], BY_ROWS), inner)
        if block == 2:
            again(layer, N.a)

    def bottom(layer):
        need(layer, N.w_qkv)

        def columns(n):
            at = span(n * 256, 256)
            R.dc[:, at] = dot(R.dp[...], R.b_w_wide[at, :], BY_COLUMNS)

        for_each(D // 256, columns)
        again(layer, N.w_up)
        need(layer, N.x)

        def rows(i):
            at = span(i * 32, 32)
            grad_in = R.dc[at, :]
            normed, factor = norm_parts(R.b_x[at, :].astype(WIDE))
            collect(layer, 0, grad_in * normed)
            collect(layer, 1, grad_in)
            grad_x = R.dy[at, :] + norm_back(grad_in * vec(layer, 0), normed, factor)
            if layer == 1:
                R.dx[at, :] = grad_x.astype(LOW)
            else:
                R.b_y[at, :] = grad_x

        for_each(SEQ // 32, rows)
        again(layer, N.x)

    def spread():
        vec_lanes, vec_group, bias_lanes, bias_group, bias_rows = small_layout(count)
        tiles = R.tiles
        tiles[...] = jnp.zeros_like(tiles)
        for layer in range(2):
            for d in range(count):
                lead = tuple((d >> (dims - 1 - i)) & 1 for i in range(dims))
                t = d // vec_group
                tiles[(layer,) + lead + (slice(0, 10),)] = grads[layer, 0:10, t * 128 : (t + 1) * 128]
            for b in range(count // 2):
                lead = tuple((b >> (dims - 2 - i)) & 1 for i in range(dims - 1))
                for i in range(bias_rows):
                    at = (b // bias_group * bias_rows + i) * 128
                    tiles[(layer,) + lead + (half, slice(10 + i, 11 + i))] = R.bias_grads[layer, 0:1, at : at + 128]

    def small_move(k):
        if k == 0:
            return remote(
                R.tiles.at[1 - core], R.tile_box.at[0], R.small_send.at[0], R.small_recv.at[0], sibling
            )
        lead = own[: k - 1] + (1 - bits[k - 1],)
        return remote(
            R.tiles.at[(core,) + lead],
            R.tile_box.at[(k,) + lead],
            R.small_send.at[k],
            R.small_recv.at[k],
            partners[k - 1],
        )

    def small_event(k):
        small_move(k).wait()
        lead = own[:k]
        view = R.tiles.at[(core,) + lead]
        view[...] = view[...] + R.tile_box[(k,) + lead]
        if k < dims:
            small_move(k + 1).start()
        else:
            pltpu.make_async_copy(view, R.g_small, R.edge_sem.at[2]).start()

    for name in (N.vecs, N.og, N.y, N.g, N.w_down, N.gp, N.w_up, N.c, N.h, N.o, N.w_out, N.q, N.k, N.v, N.p, N.x, N.a):
        load(name, 1).start()
    grads[...] = jnp.zeros_like(grads)
    edge1_local = pltpu.make_async_copy(R.s_z, R.edge1.at[1], R.edge_sem.at[0])
    edge1_remote = remote(R.s_z, R.edge1.at[0], R.edge_send.at[0], R.edge_recv.at[0], sibling)
    edge0_local = pltpu.make_async_copy(R.b_y, R.edge0.at[0], R.edge_sem.at[1])
    edge0_remote = remote(R.b_y, R.edge0.at[1], R.edge_send.at[1], R.edge_recv.at[1], sibling)

    @pl.when(core == 0)
    def _():
        edge1_remote.start()

    @pl.when(core == 1)
    def _():
        edge1_local.start()

    def compute(v):
        layer, (kind, block) = unit_of(v)
        if v >= NU:
            finished(v - NU)
        if kind == DOWN:
            if block == 0:
                top(layer)
            grad_down(layer, v, block)
            if block == 1:
                feed_back(layer)
        elif kind == UP:
            grad_up(layer, v, block)
        elif kind == OUT:
            middle(layer)
            grad_out(layer, v)
            attention_back(layer)
        else:
            grad_qkv(layer, v, block)
            if block == 2:
                bottom(layer)

    events = [(v, 1, 0, v) for v in range(total)]
    for v in range(total):
        for k in range(steps(v) + 1):
            lag = SCATTER_LAGS[k] if k < len(SCATTER_LAGS) else SCATTER_LAGS[-1] + (k - len(SCATTER_LAGS) + 1) / 8
            events.append((v + lag, 0, -k, v))
    events = sorted(events)
    tail = 0
    for key, is_compute, k, v in events:
        if is_compute:
            compute(v)
            if v == total - 1:

                @pl.when(core == 0)
                def _():
                    edge0_local.start()

                @pl.when(core == 1)
                def _():
                    edge0_remote.start()

                spread()
                small_move(0).start()
                tail = 1
        else:
            event(v, -k)
            if tail and tail <= dims + 1:
                if tail > 1:
                    small_event(tail - 2)
                tail += 1
    for k in range(max(tail - 2, 0), dims + 1):
        small_event(k)
    for v in range(NU, total):
        finished(v)

    @pl.when(core == 0)
    def _():
        edge1_remote.wait_send()
        edge0_local.wait()
        edge0_remote.wait_recv()

    @pl.when(core == 1)
    def _():
        edge1_local.wait()
        edge1_remote.wait_recv()
        edge0_remote.wait_send()

    pltpu.make_async_copy(R.tiles.at[(core,) + own], R.g_small, R.edge_sem.at[2]).wait()
    for layer in range(2):

        @pl.when(core == layer)
        def _():
            for v in range((1 - layer) * NU, (2 - layer) * NU):
                for copy in final_remote(v):
                    copy.wait_recv()


def backward(left, out_grad, lengths, dims):
    rows = D // 2**dims
    bits = (2,) * dims
    outs = dict(
        g_qkv=((rows, 3 * D), LOW),
        g_out=((rows, D), LOW),
        g_up=((2, rows, FF // 2), LOW),
        g_down=((4 * rows, D), LOW),
        g_small=((16, 128), WIDE),
        edge0=((2, SEQ, D), WIDE),
        edge1=((2, SEQ, D), WIDE),
    )
    dma = pltpu.SemaphoreType.DMA
    total = 2 * NU
    vmem = lambda shape, dtype=LOW: pltpu.VMEM(shape, dtype)
    scratch = dict(
        vecs=vmem((2, 16, D), WIDE),
        grads=vmem((2, 16, D), WIDE),
        bias_grads=vmem((2, 8, FF // 2), WIDE),
        b_og=vmem((SEQ, D)),
        b_y=vmem((SEQ, D), WIDE),
        b_w_down=vmem((FF // 2, D)),
        b_w_wide=vmem((D, 3 * D)),
        b_w_out=vmem((D, D)),
        e=vmem((2, SEQ, D)),
        dc_part=vmem((2, SEQ, D)),
        dc=vmem((SEQ, D), WIDE),
        dy=vmem((SEQ, D), WIDE),
        dx=vmem((SEQ, D)),
        f=vmem((SEQ, D)),
        do=vmem((SEQ, D)),
        dp=vmem((SEQ, 3 * D)),
        tiles=vmem((2,) + bits + (16, 128), WIDE),
        tile_box=vmem((dims + 1,) + bits + (16, 128), WIDE),
        wide_stage=vmem((2,) + bits + (rows, 512)),
        wide_box=vmem((2,) + bits + (rows, 512)),
        down_stage=vmem((2,) + bits[:-1] + (4 * rows, 256)),
        down_box=vmem((2,) + bits[:-1] + (4 * rows, 256)),
        send=dma((total, dims + 1)),
        recv=dma((total, dims + 1)),
        credit=pltpu.SemaphoreType.REGULAR((NU, dims + 1)),
        out_sem=dma((total, 2)),
        end_send=dma((total, 2)),
        end_recv=dma((total, 2)),
        load_sem=dma((len(LOADS),)),
        act_send=dma((2, 2)),
        act_recv=dma((2, 2)),
        small_send=dma((dims + 1,)),
        small_recv=dma((dims + 1,)),
        edge_sem=dma((3,)),
        edge_send=dma((2,)),
        edge_recv=dma((2,)),
    )
    for name, (shape, dtype) in saved_shapes().items():
        scratch[B + name] = vmem(shape, dtype)
    for u, (kind, block) in enumerate(BACK):
        piece = (4 * rows, 256) if kind == DOWN else (rows, 512)
        lead = bits[:-1] if kind == DOWN else bits
        scratch[HELD + str(u)] = vmem(lead + piece)
        count = dims if kind in (QKV, OUT) else dims - 1
        for k in range(1, count + 1):
            scratch[box_name(u, k)] = vmem(lead[k:] + piece)
        if kind == UP:
            scratch[box_name(u, dims)] = vmem(piece)
    names = BACK_IN + list(outs) + list(scratch)

    def kernel(*refs):
        by_name = dict(zip(names, refs))
        extra = dict(
            qkv_flat=by_name[QKV].reshape(2, D, 3 * D),
            out_flat=by_name[OUT].reshape(2, D, D),
            up_flat=by_name[UP].reshape(2, D, FF // 2),
            down_flat=by_name[DOWN].reshape(2, FF // 2, D),
        )
        backward_kernel(dims, names + list(extra), *refs, *extra.values())

    anywhere = pl.BlockSpec(memory_space=pl.ANY)
    arguments = [left[n] for n in BACK_IN[:-2]] + [out_grad, lengths]
    results = pl.pallas_call(
        kernel,
        out_shape=[jax.ShapeDtypeStruct(s, t) for s, t in outs.values()],
        in_specs=[anywhere] * (len(arguments) - 1) + [pl.BlockSpec(memory_space=pltpu.SMEM)],
        out_specs=[anywhere] * len(outs),
        scratch_shapes=list(scratch.values()),
        compiler_params=pltpu.CompilerParams(collective_id=2, has_side_effects=True, vmem_limit_bytes=62 << 20),
        name="backward",
    )(*arguments)
    return SimpleNamespace(**dict(zip(outs, results)))


def unpack_share(small, count, here):
    vec_lanes, vec_group, bias_lanes, bias_group, bias_rows = small_layout(count)
    vectors = lax.dynamic_slice(small, (0, lax.rem(here, vec_group) * vec_lanes), (10, vec_lanes))
    start = lax.rem(lax.div(here, 2), bias_group) * bias_lanes if bias_group > 1 else 0
    bias = lax.dynamic_slice(small, (10, start), (bias_rows, bias_lanes // bias_rows))
    return vectors, bias.reshape(bias_lanes)


def per_device(dims, hidden_in, lengths, out_grad, w_qkv, w_out, w_up, w_down, vectors, up_bias):
    core, here = lax.axis_index(PIPE), lax.axis_index(DP)
    count = 2**dims
    rows = D // count
    left = forward_call(dims, here, core, hidden_in, lengths, w_qkv, w_out, w_up, w_down, vectors, up_bias)
    sums = backward(left, out_grad[:, 0], lengths[:, 0], dims)
    grad_vec, grad_bias = unpack_share(sums.g_small, count, here)
    edges = jnp.where(core == 0, sums.edge0, sums.edge1)
    up = sums.g_up.reshape(2, rows, count // 2, FF // count).transpose(1, 2, 0, 3).reshape(rows, FF)
    return (
        edges[None, :, None],
        sums.g_qkv.astype(WIDE)[None],
        sums.g_out.astype(WIDE)[None],
        up.astype(WIDE)[None],
        sums.g_down.astype(WIDE)[None],
        grad_vec[None],
        grad_bias[None],
    )


def solution(mesh):
    dims = (mesh.shape[DP] - 1).bit_length()
    weights = P(PIPE, DP, None)
    placed = (
        P(None, DP, None, None),
        P(None, DP),
        P(None, DP, None, None),
        weights,
        weights,
        weights,
        weights,
        P(PIPE, None, DP),
        P(PIPE, DP),
    )
    return jax.shard_map(
        functools.partial(per_device, dims),
        mesh=mesh,
        in_specs=placed,
        out_specs=(
            P(PIPE, None, DP, None, None),
            weights,
            weights,
            weights,
            weights,
            P(PIPE, None, DP),
            P(PIPE, DP),
        ),
        check_vma=False,
    )
```

time: 1950 us -> 505 us (0.26)
  waiting for transfers between devices: 1330 us -> 0 us
  Pallas kernels: 0 us -> 488 us
  matrix products: 222 us -> 0 us
  blocking collectives: 156 us -> 0 us
  other arithmetic: 124 us -> 7.01 us
  local copies, waits for them, and re-layouts: 61.9 us -> 8.17 us
    reduce_scatter x4 -> x0, waiting for transfers between devices: 928 us -> none  [the longest x1 355 us: per_device(): lax.psum_scatter(grads_now[3], 'dp', scatter_dimension=0, tiled=True)]
    pallas_call x0 -> x2, Pallas kernels: none -> 488 us  [the longest x1 249 us: backward(): pl.pallas_call(kernel, out_shape=[jax.ShapeDtypeStruct(s, t) for s, t in...]
    all_gather x4 -> x0, waiting for transfers between devices: 302 us -> none  [the longest x1 114 us: per_device(): lax.all_gather(shards[2], 'dp', axis=1, tiled=True)]
    dot_general x46 -> x0, matrix products: 222 us -> none  [the longest x4 42.5 us: pieces(): jnp.dot(activated, w_down, preferred_element_type=jnp.float32)]
    ppermute x4 -> x0, waiting for transfers between devices: 101 us -> none  [passed_along(): lax.ppermute(value, axis, [(source, source + steps) for source in range(l...]
    all_gather x2 -> x0, blocking collectives: 81.8 us -> none  [the longest x1 45.9 us: per_device(): lax.all_gather(shards[4], 'dp', axis=2, tiled=True)]
    add x12 -> x0, other arithmetic: 80.3 us -> none  [the longest x6 75.1 us: per_device(): running = tuple((total + term for total, term in zip(running, scattered)))]
    unnamed x1 -> x0, blocking collectives: 74.5 us -> none
  transfers between devices with their start and end apart: 13 -> 0, of which waited for: 11 -> 0; matrix products, arithmetic and copies ran while one was open for 4% -> 0% of each run, Pallas kernels for 0% -> 0%
where the time goes in v2:
time: 505 us; the launch traced here: 504 us
  Pallas kernels  488 us (97%)
  local copies, waits for them, and re-layouts  8.17 us (2%)
  other arithmetic  7.01 us (1%)
    pallas_call x1, Pallas kernels, backward(): pl.pallas_call(kernel, out_shape=[jax.ShapeDtypeStruct(s, t) for s, t in...  249 us
    pallas_call x1, Pallas kernels, forward(): pl.pallas_call(kernel, out_shape=[jax.ShapeDtypeStruct(s, t) for s, t in...  239 us

profile of v2, /device:TPU:0, one launch (start us, length us, event | category | flops | bytes accessed | tf_op | source)
XLA Modules:
  0.0 503.9 jit_solution(5327391651946523778)
XLA Ops:
  0.6 0.7 reduce
  1.3 1.6 dynamic_update_slice.6
  2.9 0.0 copy-start.4
  3.0 1.4 reshape_squeeze.6
  4.4 0.1 copy.21
  4.5 1.0 reshape.33.refs_2_
  5.5 0.0 copy-done.4
  5.5 238.7 %forward.1 = (bf16[2,2,2,2,2,64,3072]{6,5,4,3,2,1,0:T(8,128)(2,1)}, bf16[2,2,2,2,2,64,1024]{6,5,4,3,2,1,0:T(8,128)(2,1)}, bf16[2,2,2,2,2,64,2048]{6,5,4,3,2,1,0:...) custom-call(bf16[64,3072]{1,0:T(8,128)(2,1)} %bitcast.43, ...), custom_call_target="tpu_custom_call" | custom-call | tf_op jit(solution)/shard_map/forward/pallas_call | solution.py:522
  244.2 249.3 %backward.1 = (bf16[64,3072]{1,0:T(8,128)(2,1)}, bf16[64,1024]{1,0:T(8,128)(2,1)}, bf16[2,64,2048]{2,1,0:T(8,128)(2,1)}, bf16[256,1024]{1,0:T(8,128)(2,1)}, f32[...) custom-call(bf16[2,2,2,2,2,64,3072]{6,5,4,3,2,1,0:T(8,128)(2,1)} %get-tuple-element.32.refs_0_, ...), custom_call_target="tpu_custom_call" | custom-call | tf_op jit(solution)/shard_map/backward/pallas_call | solution.py:1148
  493.5 0.0 copy-start.5
  493.5 0.0 copy-start.3
  493.5 0.0 copy-start.2
  493.5 0.0 copy-start.1
  493.6 3.6 select_bitcast_fusion
  497.1 0.0 copy-done.5
  497.1 0.6 dynamic_slice.7
  497.7 0.1 constant_dynamic-slice_fusion
  497.8 0.6 broadcast_in_dim.36
  498.4 0.0 copy-done.3
  498.4 0.7 bitcast_convert_fusion.2
  499.1 0.0 copy-done.2
  499.1 0.9 bitcast_convert_fusion.1
  500.0 0.0 copy-done.1
  500.0 0.1 copy.19
  500.1 0.1 bitcast_bitcast_fusion
  500.2 0.0 copy-start
  500.2 0.8 copy.17
  501.0 1.8 reshape.36
  502.9 0.0 copy-done
  502.9 1.1 bitcast_convert_fusion
  (2 shorter events, 0.0 us)
Async XLA Ops:
  2.9 2.6 copy-start.4
  493.5 3.6 copy-start.5
  493.5 4.8 copy-start.3
  493.5 5.6 %copy-start.2 = (bf16[64,3072]{1,0:T(8,128)(2,1)S(1)}, bf16[64,3072]{1,0:T(8,128)(2,1)}, u32[]{:S(2)}) copy-start(bf16[64,3072]{1,0:T(8,128)(2,1)} %get-tuple-element.52) | copy-start | bytes 1179652
  493.5 6.5 %copy-start.1 = (bf16[2,64,2048]{2,1,0:T(8,128)(2,1)S(1)}, bf16[2,64,2048]{2,1,0:T(8,128)(2,1)}, u32[]{:S(2)}) copy-start(bf16[2,64,2048]{2,1,0:T(8,128)(2,1)} %get-tuple-element.54) | copy-start | bytes 1572868
  500.2 2.6 copy-start
